TPU v7x, 128 devices: a whole 4x4x4 slice. The times are simulated.
128 devices in a mesh: dp: 8 (over x_lo, y), ctx: 8 (over x_hi, z), mod: 2 (over core).
Axes of the slice: x: 4 (x_hi: 2, x_lo: 2; x = x_hi * 2 + x_lo), y: 4, z: 4, core: 2. Of those that a mesh axis runs over, the one named last changes fastest.
Arguments:
- hidden_in: bfloat16 [8, 2048, 3584], P('dp', ('ctx', 'mod')), may hold values from -10 to 10
- out_grad: bfloat16 [8, 2048, 1792], P('dp', ('ctx', 'mod')), may hold values from -6 to 6
- modality: int32 [8, 2048], P('dp', ('ctx', 'mod')), may hold values from 0 to 1, as said below
- segment: int32 [8, 2048], P('dp'), may hold values from 0 to 2047, as said below
- w_query: bfloat16 [2, 3584, 1792], P('mod'), may hold values from -1 to 1
- w_keyval: bfloat16 [2, 3584, 512], P('mod'), may hold values from -1 to 1
Outputs:
- attended: bfloat16 [8, 2048, 1792], P('dp', ('ctx', 'mod'))
- grad_hidden: bfloat16 [8, 2048, 3584], P('dp', ('ctx', 'mod'))
- grad_query_w: bfloat16 [2, 3584, 1792], P('mod', ('dp', 'ctx'))
- grad_keyval_w: bfloat16 [2, 3584, 512], P('mod', ('dp', 'ctx'))
Inputs may be any that keep to these rules, and one draw needn't show every extreme that they name: Each aligned block of 128 positions holds one modality; the last block of each lane is text. Each position holds the first position of its segment, so it never falls along a lane and starts at 0; every text position starts a segment of its own; a latent segment is a run of whole latent blocks.
All inputs are finite; a program needn't handle non-finite values.
Results may differ from a plain program's by a relative error of at most 0.04.
Values may be sent and summed in bfloat16 or wider, within the bound.
A program may use at most 128 MiB of HBM per device.

v0:
```python
import math

import jax
import jax.numpy as jnp
from jax import lax
from jax.sharding import PartitionSpec as P

HS = 128
BLOCK = 128


masked_low = -1e30


def block_ranks(block_mod):
    block_total = block_mod.shape[0]
    order = jnp.arange(block_total, dtype=jnp.int32)
    same = (block_mod[:, None] == block_mod[None, :]) & (order[None, :] < order[:, None])
    return jnp.sum(same.astype(jnp.int32), axis=1)


def pack_blocks(values, block_mod, slot_rank):
    block_total = block_mod.shape[0]
    target = jnp.arange(2, dtype=jnp.int32)[:, None, None]
    slot_ids = jnp.arange(block_total, dtype=jnp.int32)[None, :, None]
    select = ((block_mod[None, None, :] == target) & (slot_rank[None, None, :] == slot_ids)).astype(
        values.dtype
    )
    return jnp.einsum("jsb,brc->jsrc", select, values, preferred_element_type=jnp.float32).astype(
        values.dtype
    )


def unpack_blocks(buffers, block_mod, slot_rank):
    block_total = block_mod.shape[0]
    flat = buffers.reshape((2 * block_total,) + buffers.shape[2:])
    return jnp.take(flat, block_mod * block_total + slot_rank, axis=0)


def score_block(queries, key_rows, seg_query, seg_keys, score_scale):
    scores = (
        jnp.einsum("rgjd,ngd->gjrn", queries, key_rows, preferred_element_type=jnp.float32)
        * score_scale
    )
    allowed = seg_keys[None, :] <= seg_query[:, None]
    return (scores, allowed)


def key_terms(queries, grad_out, lane_block, seg_query, seg_keys, log_total, delta, score_scale):
    scores, allowed = score_block(queries, lane_block[:, 0], seg_query, seg_keys, score_scale)
    prob = jnp.where(allowed, jnp.exp(scores - log_total[..., None]), 0.0)
    dprob = jnp.einsum(
        "rgjd,ngd->gjrn", grad_out, lane_block[:, 1], preferred_element_type=jnp.float32
    )
    dscore = (prob * (dprob - delta[..., None])).astype(jnp.bfloat16)
    return (prob, dscore)


def key_side(prob, dscore, queries, grad_out, score_scale):
    grad_k = (
        jnp.einsum("gjrn,rgjd->ngd", dscore, queries, preferred_element_type=jnp.float32)
        * score_scale
    )
    grad_v = jnp.einsum(
        "gjrn,rgjd->ngd", prob.astype(jnp.bfloat16), grad_out, preferred_element_type=jnp.float32
    )
    stacked = jnp.stack([grad_k, grad_v], axis=1)
    return stacked.reshape(stacked.shape[0], -1)


def on_device(hidden_in, out_grad, modality, segment, w_query, w_keyval):
    row_count = hidden_in.shape[1]
    model_width = hidden_in.shape[2]
    query_width = w_query.shape[2]
    pair_width = w_keyval.shape[2]
    key_width = pair_width // 2
    block_total = row_count // BLOCK
    groups = key_width // HS
    per_group = query_width // key_width
    score_scale = 1.0 / math.sqrt(HS)
    core_count = lax.axis_size("mod")
    lane_length = row_count * lax.axis_size("ctx") * core_count
    key_block = math.gcd(lane_length, 512)
    w_both = jnp.concatenate([w_query[0], w_keyval[0]], axis=1)
    block_mod = modality[0].reshape(block_total, BLOCK)[:, 0]
    slot_rank = block_ranks(block_mod)
    packed = pack_blocks(
        hidden_in[0].reshape(block_total, BLOCK, model_width), block_mod, slot_rank
    )
    block_items = lax.all_to_all(packed, "mod", split_axis=0, concat_axis=0, tiled=True)
    made_rows = jnp.einsum("sbrd,dc->sbrc", block_items, w_both, preferred_element_type=jnp.float32)
    received, made_rows = (block_items, made_rows.astype(jnp.bfloat16))
    returned = lax.all_to_all(made_rows, "mod", split_axis=0, concat_axis=0, tiled=True)
    projected = unpack_blocks(returned, block_mod, slot_rank).reshape(
        row_count, query_width + pair_width
    )
    queries = projected[:, :query_width].reshape(row_count, groups, per_group, HS)
    lane_keys = lax.all_gather(
        projected[:, query_width:], ("ctx", "mod"), axis=0, tiled=True
    ).reshape(lane_length, 2, groups, HS)
    offset = (lax.axis_index("ctx") * core_count + lax.axis_index("mod")) * row_count
    seg_all = segment[0]
    seg_query = lax.dynamic_slice_in_dim(seg_all, offset, row_count, 0)

    def forward_step(block_index, running):
        row_top, weight_sum, weighted = running
        first_row = block_index * key_block
        lane_block = lax.dynamic_slice_in_dim(lane_keys, first_row, key_block, 0)
        seg_keys = lax.dynamic_slice_in_dim(seg_all, first_row, key_block, 0)
        scores, allowed = score_block(queries, lane_block[:, 0], seg_query, seg_keys, score_scale)
        new_top = jnp.maximum(row_top, jnp.max(jnp.where(allowed, scores, masked_low), axis=-1))
        weights = jnp.where(allowed, jnp.exp(scores - new_top[..., None]), 0.0)
        fade = jnp.exp(row_top - new_top)
        weight_sum = weight_sum * fade + jnp.sum(weights, axis=-1)
        weighted = weighted * fade[..., None] + jnp.einsum(
            "gjrn,ngd->gjrd",
            weights.astype(jnp.bfloat16),
            lane_block[:, 1],
            preferred_element_type=jnp.float32,
        )
        return (new_top, weight_sum, weighted)

    start_top = jnp.full((groups, per_group, row_count), masked_low, jnp.float32)
    start_sum = jnp.zeros((groups, per_group, row_count), jnp.float32)
    start_weighted = jnp.zeros((groups, per_group, row_count, HS), jnp.float32)
    row_top, weight_sum, weighted = lax.fori_loop(
        0, lane_length // key_block, forward_step, (start_top, start_sum, start_weighted)
    )
    attended = (
        jnp.transpose(weighted / weight_sum[..., None], (2, 0, 1, 3))
        .reshape(row_count, query_width)
        .astype(jnp.bfloat16)
    )
    log_total = row_top + jnp.log(weight_sum)
    grad_out = out_grad[0].reshape(row_count, groups, per_group, HS)
    delta = jnp.einsum(
        "rgjd,rgjd->gjr",
        grad_out,
        attended.reshape(row_count, groups, per_group, HS),
        preferred_element_type=jnp.float32,
    )
    start_dq = jnp.zeros((row_count, groups, per_group, HS), jnp.float32)

    def grad_step(block_index, running):
        grad_q, key_grads = running
        first_row = block_index * key_block
        lane_block = lax.dynamic_slice_in_dim(lane_keys, first_row, key_block, 0)
        seg_keys = lax.dynamic_slice_in_dim(seg_all, first_row, key_block, 0)
        prob, dscore = key_terms(
            queries, grad_out, lane_block, seg_query, seg_keys, log_total, delta, score_scale
        )
        grad_q = grad_q + jnp.einsum(
            "gjrn,ngd->rgjd", dscore, lane_block[:, 0], preferred_element_type=jnp.float32
        )
        key_part = key_side(prob, dscore, queries, grad_out, score_scale)
        key_grads = lax.dynamic_update_slice_in_dim(key_grads, key_part, first_row, 0)
        return (grad_q, key_grads)

    grad_q, key_grads = lax.fori_loop(
        0,
        lane_length // key_block,
        grad_step,
        (start_dq, jnp.zeros((lane_length, pair_width), jnp.float32)),
    )
    grad_kv = lax.psum_scatter(
        key_grads.astype(jnp.bfloat16), ("ctx", "mod"), scatter_dimension=0, tiled=True
    )
    grad_q = (grad_q * score_scale).astype(jnp.bfloat16).reshape(row_count, query_width)
    grads_home = jnp.concatenate([grad_q, grad_kv], axis=1)
    grad_packed = pack_blocks(
        grads_home.reshape(block_total, BLOCK, query_width + pair_width), block_mod, slot_rank
    )
    block_items = lax.all_to_all(grad_packed, "mod", split_axis=0, concat_axis=0, tiled=True)
    spread = jnp.einsum("sbrc,dc->sbrd", block_items, w_both, preferred_element_type=jnp.float32)
    grad_items, spread = (block_items, spread.astype(jnp.bfloat16))
    spread_home = lax.all_to_all(spread, "mod", split_axis=0, concat_axis=0, tiled=True)
    grad_hidden = unpack_blocks(spread_home, block_mod, slot_rank)
    flat_tokens = received.reshape(-1, model_width)
    flat_grads = grad_items.reshape(-1, query_width + pair_width)
    partial_sum = lax.dot_general(
        flat_tokens, flat_grads, (((0,), (0,)), ((), ())), preferred_element_type=jnp.float32
    )
    lane_count = lax.axis_size("dp")
    part_count = lax.axis_size("ctx")
    partial_sum = partial_sum.reshape(
        lane_count, part_count, model_width // (lane_count * part_count), query_width + pair_width
    )
    summed = lax.psum_scatter(
        partial_sum.astype(jnp.bfloat16), "dp", scatter_dimension=0, tiled=True
    ).astype(jnp.float32)
    summed = lax.psum_scatter(
        summed.astype(jnp.bfloat16), "ctx", scatter_dimension=1, tiled=True
    ).astype(jnp.float32)
    weight_grad = summed[0, 0].astype(jnp.bfloat16)
    return (
        attended[None],
        grad_hidden,
        weight_grad[None, :, :query_width],
        weight_grad[None, :, query_width:],
    )


def solution(mesh):
    return jax.shard_map(
        on_device,
        mesh=mesh,
        in_specs=(
            P("dp", ("ctx", "mod"), None),
            P("dp", ("ctx", "mod"), None),
            P("dp", ("ctx", "mod")),
            P("dp", None),
            P("mod", None, None),
            P("mod", None, None),
        ),
        out_specs=(
            P("dp", ("ctx", "mod"), None),
            P("dp", ("ctx", "mod"), None),
            P("mod", ("dp", "ctx"), None),
            P("mod", ("dp", "ctx"), None),
        ),
        check_vma=False,
    )
```

profile of v0, /device:TPU:1, one launch (start us, length us, event | category | flops | bytes accessed | tf_op | source)
XLA Modules:
  0.0 521.9 jit_solution(18146914223508744014)
XLA Ops:
  9.5 6.5 %all_to_all.20 = bf16[2,1,128,3584]{3,2,1,0:T(8,128)(2,1)S(1)} all-to-all(bf16[2,1,128,3584]{3,2,1,0:T(8,128)(2,1)S(1)} %fusion.46), channel_id=1, replica_groups=mesh['dp'=8,'ctx'=8,'mod'=2] {'mod'}, dimensions={0} | all-to-all | bytes 3670016 | tf_op jit(solution)/shard_map/all_to_all | solution.py:90
  17.3 11.2 %fusion.45 = bf16[2,1,128,2304]{3,2,1,0:T(8,128)(2,1)} fusion(bf16[3584,512]{1,0:T(8,128)(2,1)S(1)} %bitcast.240, bf16[3584,1792]{1,0:T(8,128)(2,1)} %bitcast.237, bf16[2,1,128,3584]{3,2,1,0:T(8,128)(2,1)S(1)} %all_to_all.20), kind=kOutput, calls=%fused_computation.59 | convolution fusion | flops 4261478400 | bytes 19529728 | tf_op jit(solution)/shard_map/sbrd,dc->sbrc/dot_general | solution.py:91
  28.6 4.0 all-to-all-start.1
  38.1 47.7 %all-gather.2.cloned.1.call-done = bf16[2048,512]{0,1:T(8,128)(2,1)} async-done(((bf16[128,512]{0,1:T(8,128)(2,1)}), bf16[2048,512]{0,1:T(8,128)(2,1)}) %all-gather.2.cloned.1.call-update) | async-done | bytes 2097168 | tf_op jit(solution)/shard_map/all_gather | solution.py:98
  85.8 3.9 copy.52
  89.7 39.6 %while.36 = (s32[]{:T(128)}, f32[2,7,128]{2,1,0:T(8,128)S(1)}, f32[2,7,128]{2,1,0:T(8,128)S(1)}, f32[2,7,128,128]{3,2,1,0:T(8,128)S(1)}, s32[2048]{0:T(1024)S(1)...) while((s32[]{:T(128)}, f32[2,7,128]{2,1,0:T(8,128)S(1)}, ...), condition=%wide.region_3.4_spmd.clone, body=%wide.region_0.3_spmd.clone.sunk | while | flops 480617216 | bytes 14211795 | solution.py:126
  89.9 3.4 fusion.84
  96.1 3.4 fusion.87
  106.0 3.4 fusion.87
  115.9 3.4 fusion.87
  125.8 3.4 fusion.87
  133.1 49.7 %while.37 = (s32[]{:T(128)}, f32[128,2,7,128]{0,3,2,1:T(8,128)S(1)}, bf16[2048,512]{0,1:T(8,128)(2,1)}, bf16[2048,2,2,128]{3,0,2,1:T(8,128)(2,1)}, s32[2048]{0:T...) while((s32[]{:T(128)}, ...), condition=%wide.region_5.6_spmd.clone, body=%wide.region_4.5_spmd.clone.sunk | while | flops 1184628736 | bytes 38498052 | solution.py:159
  136.7 3.6 fusion.96
  149.1 3.6 fusion.96
  161.5 3.6 fusion.96
  174.0 3.6 fusion.96
  182.8 3.9 copy.86
  190.9 62.9 %reduce-scatter.10.cloned.1.call-done = bf16[128,512]{1,0:T(8,128)(2,1)} async-done(((bf16[2048,512]{1,0:T(8,128)(2,1)}), bf16[128,512]{1,0:T(8,128)(2,1)}) %reduce-scatter.10.cloned.1.call-update) | async-done | bytes 131088 | tf_op jit(solution)/shard_map/reduce_scatter | solution.py:165
  255.1 6.9 %all_to_all.21 = bf16[2,1,128,2304]{3,2,1,0:T(8,128)(2,1)S(1)} all-to-all(bf16[2,1,128,2304]{3,2,1,0:T(8,128)(2,1)S(1)} %fusion.48), channel_id=1, replica_groups=mesh['dp'=8,'ctx'=8,'mod'=2] {'mod'}, dimensions={0} | all-to-all | bytes 2359296 | tf_op jit(solution)/shard_map/all_to_all | solution.py:173
  262.0 8.0 %convolution_convert_fusion = bf16[8,8,56,2304]{3,2,1,0:T(8,128)(2,1)} fusion(bf16[8,8,56,256]{3,2,1,0:T(8,128)(2,1)S(1)} %bitcast.223, bf16[256,2304,1,1]{1,0,3,2:T(8,128)(2,1)S(1)} %bitcast.225), kind=kOutput, calls=%fused_computation.52 | convolution fusion | flops 4236115968 | bytes 19529728 | tf_op jit(solution)/shard_map/dot_general | solution.py:180
  270.1 167.7 %reduce-scatter.6.cloned.1.call-done = bf16[1,8,56,2304]{3,2,1,0:T(8,128)(2,1)} async-done(((bf16[8,8,56,2304]{3,2,1,0:T(8,128)(2,1)}), bf16[1,8,56,2304]{3,2,1,0:T(8,128)(2,1)}) %reduce-scatter.6.cloned.1.call-update) | async-done | bytes 2064400 | tf_op jit(solution)/shard_map/reduce_scatter | solution.py:188
  438.8 8.1 %fusion.43 = bf16[2,1,128,3584]{3,2,1,0:T(8,128)(2,1)S(1)} fusion(bf16[3584,512]{1,0:T(8,128)(2,1)} %bitcast.239, bf16[3584,1792]{1,0:T(8,128)(2,1)} %bitcast.238, bf16[2,1,128,2304]{3,2,1,0:T(8,128)(2,1)S(1)} %all_to_all.21), kind=kOutput, calls=%fused_computation.57 | convolution fusion | flops 4261806080 | bytes 19529728 | tf_op jit(solution)/shard_map/sbrc,dc->sbrd/dot_general | solution.py:174
  446.9 5.4 %all_to_all.22 = bf16[2,1,128,3584]{3,2,1,0:T(8,128)(2,1)S(1)} all-to-all(bf16[2,1,128,3584]{3,2,1,0:T(8,128)(2,1)S(1)} %fusion.43), channel_id=1, replica_groups=mesh['dp'=8,'ctx'=8,'mod'=2] {'mod'}, dimensions={0} | all-to-all | bytes 3670016 | tf_op jit(solution)/shard_map/all_to_all | solution.py:176
  453.3 59.0 %reduce-scatter.8.cloned.1.call-done = bf16[1,1,56,2304]{3,2,1,0:T(8,128)(2,1)} async-done(((bf16[1,8,56,2304]{3,2,1,0:T(8,128)(2,1)}), bf16[1,1,56,2304]{3,2,1,0:T(8,128)(2,1)}) %reduce-scatter.8.cloned.1.call-update) | async-done | bytes 258064 | tf_op jit(solution)/shard_map/reduce_scatter | solution.py:191
  (115 shorter events, 80.8 us)
Async XLA Ops:
  9.2 8.1 %copy-start.5 = (bf16[1,3584,512]{2,1,0:T(8,128)(2,1)S(1)}, bf16[1,3584,512]{2,1,0:T(8,128)(2,1)}, u32[]{:S(2)}) copy-start(bf16[1,3584,512]{2,1,0:T(8,128)(2,1)} %param.15) | copy-start | bytes 11010052
  16.0 1.3 copy-start.1
  17.3 15.2 %copy-start.4 = (s32[1,128]{1,0:T(1,128)S(1)}, s32[1,128]{1,0:T(1,128)}, u32[]{:S(2)}) copy-start(s32[1,128]{1,0:T(1,128)} %param.12) | copy-start | bytes 1540
  28.6 5.8 %all-to-all-start.1 = ((bf16[2,1,128,2304]{3,2,1,0:T(8,128)(2,1)}), bf16[2,1,128,2304]{3,2,1,0:T(8,128)(2,1)S(1)}, u32[]{:S(2)}, u32[]{:S(2)}) async-start(bf16[2,1,128,2304]{3,2,1,0:T(8,128)(2,1)} %fusion.45), calls=%async_computation.1 | async-start | bytes 2359296 | tf_op jit(solution)/shard_map/all_to_all | solution.py:93
  32.5 5.5 %copy-start.3 = (s32[1,2048]{1,0:T(1,128)S(1)}, s32[1,2048]{1,0:T(1,128)}, u32[]{:S(2)}) copy-start(s32[1,2048]{1,0:T(1,128)} %param.13) | copy-start | bytes 24580
  32.5 53.2 %all-gather.2.cloned.1.call-start = ((), (), s32[]{:S(2)}) async-start(), calls=%async_computation.7 | async-start | bytes 2228224 | tf_op jit(solution)/shard_map/all_gather | solution.py:98
  35.5 218.3 %reduce-scatter.10.cloned.1.call-start = ((), (), s32[]{:S(2)}) async-start(), calls=%async_computation.10 | async-start | bytes 2228224 | tf_op jit(solution)/shard_map/reduce_scatter | solution.py:165
  136.7 4.3 copy-start
  149.1 4.3 copy-start
  161.5 4.3 copy-start
  174.0 4.3 copy-start
  186.8 251.0 %reduce-scatter.6.cloned.1.call-start = ((), (), s32[]{:S(2)}) async-start(), calls=%async_computation.8 | async-start | bytes 18579456 | tf_op jit(solution)/shard_map/reduce_scatter | solution.py:188
  270.0 167.8 %copy-start.2 = (bf16[2,7,128,128]{2,3,1,0:T(8,128)(2,1)S(1)}, bf16[2,7,128,128]{2,3,1,0:T(8,128)(2,1)}, u32[]{:S(2)}) copy-start(bf16[2,7,128,128]{2,3,1,0:T(8,128)(2,1)} %get-tuple-element.503) | copy-start | bytes 1376260
  270.0 242.3 %reduce-scatter.8.cloned.1.call-start = ((), (), s32[]{:S(2)}) async-start(), calls=%async_computation.9 | async-start | bytes 2322432 | tf_op jit(solution)/shard_map/reduce_scatter | solution.py:191
Sparse Core Ops, SparseCore 0:
  36.2 49.5 all-gather.1
  186.9 66.8 reduce-scatter.9
  270.1 167.5 reduce-scatter.5
  441.4 70.8 reduce-scatter.7
where the time goes:
time: 524 us; the launch traced here: 522 us
  waiting for transfers between devices  339 us (65%)
  matrix products  99.4 us (19%)
  local copies, waits for them, and re-layouts  26.4 us (5%)
  other arithmetic  19.3 us (4%)
  blocking collectives  18.8 us (4%)
  between operations  14.1 us (3%)
    reduce_scatter x1, waiting for transfers between devices, on_device(): lax.psum_scatter(partial_sum.astype(jnp.bfloat16), 'dp', scatter_dimensio...  168 us
    reduce_scatter x1, waiting for transfers between devices, on_device(): lax.psum_scatter(key_grads.astype(jnp.bfloat16), ('ctx', 'mod'), scatter_...  62.9 us
    reduce_scatter x1, waiting for transfers between devices, on_device(): lax.psum_scatter(summed.astype(jnp.bfloat16), 'ctx', scatter_dimension=1,...  59 us
    all_gather x1, waiting for transfers between devices, on_device(): lax.all_gather(projected[:, query_width:], ('ctx', 'mod'), axis=0, tiled=...  47.7 us
    dot_general x8, matrix products, score_block(): jnp.einsum('rgjd,ngd->gjrn', queries, key_rows, preferred_element_type=jn...  27.1 us
    dot_general x4, matrix products, key_terms(): jnp.einsum('rgjd,ngd->gjrn', grad_out, lane_block[:, 1], preferred_elemen...  14.3 us
    dot_general x4, matrix products, forward_step(): jnp.einsum('gjrn,ngd->gjrd', weights.astype(jnp.bfloat16), lane_block[:,...  13.7 us
    unnamed x16, local copies, waits for them, and re-layouts  12.7 us
  transfers between devices with their start and end apart: 5, of which 5 were waited for; matrix products, arithmetic and copies ran while one was open for 3% of the time, Pallas kernels for 0%

commit v1 on v0

v1 whole, which is shorter than its diff:
```python
import functools
import math

import jax
import jax.numpy as jnp
from jax import lax
from jax.experimental import pallas as pl
from jax.experimental.pallas import tpu as pltpu
from jax.sharding import PartitionSpec as P

HS = 128
BLOCK = 128
D = 3584
QW = 1792
KW = 256
SEQ = 2048
HEADS = 7
GW = HEADS * HS
CHIP = 2 * BLOCK
SLICE = 448
PART = 56
MESH = pl.DeviceIdType.MESH
BF = jnp.bfloat16
F32 = jnp.float32


def aligned(index, step):
    return pl.multiple_of(index * step, step)


def dot(a, b, dims=((1,), (0,))):
    return lax.dot_general(a, b, (dims, ((), ())), preferred_element_type=F32)


def send(src, dst, send_sem, recv_sem, **device):
    return pltpu.make_async_remote_copy(
        src_ref=src, dst_ref=dst, send_sem=send_sem, recv_sem=recv_sem,
        device_id=device, device_id_type=MESH,
    )


def arrived(dst, sem):
    pltpu.make_async_copy(dst, dst, sem).wait()


def layer(
    hid, og, modv, segv, wq, wkv,
    att_o, gh_o, gwq_o, gwkv_o,
    wq_v, wkv_v, hidf, hid_t, ogf, mods, at, kvs, kvr, kvall, qs, qr, qf, bias,
    attb, attf, dqb, gq, acc, dkvb, dkr, dkx, dkxr, gkv, bg, be, cf, cs, crz, cx, cxr, keep, fin, finr, sb, sr,
    w_sem, pair_s, pair_r, mod_s, mod_r, a_s, a_r, af_s, af_r, kv_s, kv_r,
    att_s, att_r, gq_s, gq_r, b_s, b_r, dk_s, dk_r, c_s, c_r, cx_s, cx_r, fin_s, fin_r,
):
    dp, ctx, core = lax.axis_index("dp"), lax.axis_index("ctx"), lax.axis_index("mod")
    xlo, y, xhi, z = dp // 4, dp % 4, ctx // 4, ctx % 4
    other = 1 - core
    here = dp * 2 + core
    expert = core.astype(F32)
    scale = 1.0 / math.sqrt(HS)

    q_cols = []
    for group in (other, core):
        for first, width in ((0, 512), (512, 384)):
            q_cols.append((group, first, width))
    loads = [pltpu.make_async_copy(wkv, wkv_v, w_sem.at[0])]
    for i, (group, first, width) in enumerate(q_cols):
        cols = pl.ds(pl.multiple_of(group * GW + first, 128), width)
        loads.append(pltpu.make_async_copy(wq.at[:, cols], wq_v.at[:, cols], w_sem.at[1 + i]))
    for load in loads:
        load.start()

    barrier = pltpu.get_barrier_semaphore()
    for k in range(8):
        pl.semaphore_signal(barrier, inc=1, device_id={"dp": (dp + k) % 8, "mod": other}, device_id_type=MESH)
        if k:
            pl.semaphore_signal(barrier, inc=1, device_id={"dp": (dp + k) % 8}, device_id_type=MESH)
            pl.semaphore_signal(barrier, inc=1, device_id={"ctx": (ctx + k) % 8}, device_id_type=MESH)
    pl.semaphore_wait(barrier, 22)

    own_rows = pl.ds(aligned(core, BLOCK), BLOCK)
    other_rows = pl.ds(aligned(other, BLOCK), BLOCK)
    sent = []

    hid_copy = send(hid, hidf.at[own_rows], pair_s.at[0], pair_r.at[0], mod=other)
    hid_copy.start()
    og_copy = send(og.at[:, pl.ds(aligned(other, GW), GW)], ogf.at[own_rows], pair_s.at[1], pair_r.at[1], mod=other)
    og_copy.start()
    sent += [hid_copy, og_copy]
    mods[here] = modv[...]
    for k in range(8):
        for c in range(2):
            if k == 0 and c == 0:
                continue
            dev = {"dp": (dp + k) % 8, "mod": other if c else core}
            copy = send(modv, mods.at[here], mod_s.at[k, c], mod_r.at[k, c], **dev)
            copy.start()
            sent.append(copy)
    hidf[own_rows, :] = hid[...]
    ogf[own_rows, :] = og[:, pl.ds(aligned(core, GW), GW)]

    here_lanes = pl.ds(aligned(here, BLOCK), BLOCK)
    for i in range(7):
        hid_t[i * 512:(i + 1) * 512, :] = hid[:, i * 512:(i + 1) * 512].T
    for k in (5, 1, 6, 3, 4, 2, 7):
        to = (dp + k) % 8
        for s in range(2):
            rows = pl.ds(pl.multiple_of((s * 4 + to % 4) * SLICE, 64), SLICE)
            copy = send(
                hid_t.at[rows], at.at[pl.ds(s * SLICE, SLICE), here_lanes], a_s.at[k, s], a_r.at[k, s], dp=to
            )
            copy.start()
            sent.append(copy)
    for s in range(2):
        rows = pl.ds(pl.multiple_of((s * 4 + y) * SLICE, 64), SLICE)
        at[s * SLICE:(s + 1) * SLICE, here_lanes] = hid_t[rows, :]

    hid_copy.wait_recv()
    loads[0].wait()
    made = dot(hidf[...], wkv_v[...]).astype(BF)
    for i in range(2):
        for g in range(2):
            kvs[i, g] = made[:, (i * 2 + g) * HS:(i * 2 + g + 1) * HS]
    copy = send(kvs.at[:, other], kvr, pair_s.at[2], pair_r.at[2], mod=other)
    copy.start()
    sent.append(copy)
    for k in range(8):
        for c in range(2):
            if k or c:
                arrived(mods.at[(dp - k + 8) % 8 * 2 + (other if c else core)], mod_r.at[k, c])
    mine = [
        jnp.broadcast_to(mods[dp * 2 + b][0:1, :], (BLOCK, HS)) == expert for b in range(2)
    ]
    copy.wait_recv()
    for i in range(2):
        for b in range(2):
            rows = slice(b * BLOCK, (b + 1) * BLOCK)
            kvall[i, pl.ds(pl.multiple_of(ctx * CHIP + b * BLOCK, BLOCK), BLOCK), :] = jnp.where(
                mine[b], kvs[i, core, rows, :], kvr[i, rows, :]
            )
    ctx_rows = pl.ds(aligned(ctx, CHIP), CHIP)
    xctx = (1 - xhi) * 4 + z
    xctx_rows = pl.ds(aligned(xctx, CHIP), CHIP)
    copy = send(kvall.at[:, ctx_rows], kvall.at[:, ctx_rows], kv_s.at[0, 0], kv_r.at[0, 0], ctx=xctx)
    copy.start()
    sent.append(copy)
    for k in (1, 3, 2):
        copy = send(
            kvall.at[:, ctx_rows], kvall.at[:, ctx_rows], kv_s.at[0, k], kv_r.at[0, k], ctx=xhi * 4 + (z + k) % 4
        )
        copy.start()
        sent.append(copy)

    def project(i):
        group, first, width = q_cols[i]
        loads[1 + i].wait()
        cols = pl.ds(pl.multiple_of(group * GW + first, 128), width)
        qs[group, :, first:first + width] = dot(hidf[...], wq_v[:, cols]).astype(BF)

    project(0)
    arrived(kvall.at[:, xctx_rows], kv_r.at[0, 0])
    for k in (1, 3, 2):
        copy = send(
            kvall.at[:, xctx_rows], kvall.at[:, xctx_rows], kv_s.at[1, k], kv_r.at[1, k], ctx=xhi * 4 + (z + k) % 4
        )
        copy.start()
        sent.append(copy)
    project(1)
    q_copy = send(qs.at[other], qr, pair_s.at[3], pair_r.at[3], mod=other)
    q_copy.start()
    sent.append(q_copy)
    project(2)
    project(3)
    seg_rows = segv[:, pl.ds(aligned(ctx, CHIP), CHIP)]
    seg_col = jnp.broadcast_to(seg_rows[0:1, :], (128, CHIP)).T[:, 0:1]
    bias[...] = jnp.where(segv[0:1, :] <= seg_col, 0.0, -1e30)
    acc[...] = jnp.zeros_like(acc)
    q_copy.wait_recv()
    for b in range(2):
        rows = slice(b * BLOCK, (b + 1) * BLOCK)
        pick = jnp.broadcast_to(mods[dp * 2 + b][0:1, 0:1], (BLOCK, GW)) == expert
        qf[rows, :] = jnp.where(pick, qs[core, rows, :], qr[rows, :])
    og_copy.wait_recv()
    for k in (1, 3, 2):
        for part, half in enumerate((xhi, 1 - xhi)):
            rows = pl.ds(aligned(half * 4 + (z - k + 4) % 4, CHIP), CHIP)
            arrived(kvall.at[:, rows], kv_r.at[part, k])

    def forward_hidden(k):
        lanes = pl.ds(pl.multiple_of(((dp - k + 8) % 8 * 2 + core) * BLOCK, BLOCK), BLOCK)
        copy = send(at.at[:, lanes], at.at[:, lanes], af_s.at[k], af_r.at[k], mod=other)
        return copy

    def one_head(i, carry):
        slot, target = i // 2, i % 2
        head = target * 4 + slot
        lanes = pl.ds(aligned(head, HS), HS)
        full_lanes = pl.ds(aligned(core * HEADS + head, HS), HS)
        q, go = qf[:, lanes], ogf[:, lanes]
        keys, values = kvall[0], kvall[1]
        scores = dot(q, keys, ((1,), (1,))) * (scale * math.log2(math.e)) + bias[...]
        top = jnp.max(scores, axis=1, keepdims=True)
        weights = jnp.exp2(scores - top)
        total = jnp.sum(weights, axis=1, keepdims=True)
        low = weights.astype(BF)
        inv = 1.0 / total
        attended = (dot(low, values) * inv).astype(BF)
        attb[head] = attended
        copy = send(
            attb.at[head, other_rows], attf.at[:, full_lanes], att_s.at[head], att_r.at[head], mod=other
        )
        copy.start()
        attf[:, full_lanes] = attb[head, own_rows, :]
        go32 = go.astype(F32)
        delta = jnp.sum(go32 * attended.astype(F32), axis=1, keepdims=True)
        dprob = dot(go, values, ((1,), (1,)))
        dscore = (weights * (dprob * inv - delta * inv)).astype(BF)
        dq = (dot(dscore, keys) * scale).astype(BF)
        dqb[head] = dq
        gq[:, full_lanes] = dq
        copy = send(dqb.at[head], gq.at[:, full_lanes], gq_s.at[head], gq_r.at[head], mod=other)
        copy.start()
        send_grads(dqb.at[head], target, slot, b_s.at[head])
        acc[0] += dot(q.T, dscore)
        acc[1] += dot((go32 * inv).astype(BF).T, low)
        return carry

    def grads_copy(src, target, slot, sems, k):
        rows = pl.ds(aligned(dp, CHIP), CHIP)
        return send(
            src, bg.at[slot, rows], sems.at[k], b_r.at[slot, dp], dp=core * 4 + (y + k) % 4, mod=target
        )

    def send_grads(src, target, slot, sems):
        at_home = jnp.logical_and(xlo == core, target == core)
        rows = pl.ds(aligned(dp, CHIP), CHIP)
        for k in (1, 3, 2):
            grads_copy(src, target, slot, sems, k).start()

        @pl.when(at_home)
        def _():
            pltpu.make_async_copy(src, bg.at[slot, rows], b_r.at[slot, dp]).start()

        @pl.when(jnp.logical_not(at_home))
        def _():
            grads_copy(src, target, slot, sems, 0).start()

    def grads_sent(src, target, slot, sems):
        at_home = jnp.logical_and(xlo == core, target == core)
        for k in (1, 3, 2):
            grads_copy(src, target, slot, sems, k).wait_send()

        @pl.when(jnp.logical_not(at_home))
        def _():
            grads_copy(src, target, slot, sems, 0).wait_send()

    lax.fori_loop(0, 4, one_head, 0)
    for k in range(8):
        if k:
            lanes = pl.ds(pl.multiple_of(((dp - k + 8) % 8 * 2 + core) * BLOCK, BLOCK), BLOCK)
            for s in range(2):
                arrived(at.at[pl.ds(s * SLICE, SLICE), lanes], a_r.at[k, s])
        copy = forward_hidden(k)
        copy.start()
        sent.append(copy)
    lax.fori_loop(4, HEADS, one_head, 0)

    for c in range(8):
        for i in range(2):
            dkvb[c // 4, c % 4, i] = acc[i, :, c * CHIP:(c + 1) * CHIP].astype(BF)
    for k in (1, 3, 2):
        to = (z + k) % 4
        copy = send(dkvb.at[:, to], dkr.at[k - 1], dk_s.at[k], dk_r.at[k], ctx=xhi * 4 + to)
        copy.start()
        sent.append(copy)

    for k in range(8):
        lanes = pl.ds(pl.multiple_of(((dp - k + 8) % 8 * 2 + other) * BLOCK, BLOCK), BLOCK)
        arrived(at.at[:, lanes], af_r.at[k])

    def weight_block(slot, carry):
        for source in range(8):
            arrived(bg.at[slot, pl.ds(source * CHIP, CHIP)], b_r.at[slot, source])
        for t in range(16):
            rows = slice(t * BLOCK, (t + 1) * BLOCK)
            kind = mods[t][0:1, :]
            block = bg[slot, rows, :]
            second = jnp.where(jnp.broadcast_to(kind, (BLOCK, HS)) == 1.0, block, jnp.zeros_like(block))
            be[rows, HS:] = second
            be[rows, :HS] = block - second
        cf[...] = dot(at[...], be[...])
        for c in range(8):
            for e in range(2):
                cols = slice(e * HS, (e + 1) * HS)
                both = jnp.concatenate(
                    [cf[c * PART:(c + 1) * PART, cols], cf[SLICE + c * PART:SLICE + (c + 1) * PART, cols]], axis=0
                )
                cs[slot, c % 4, c // 4, e] = both.astype(BF)
        for k in (1, 3, 2):
            to = (z + k) % 4
            send(cs.at[slot, to], crz.at[slot, k - 1], c_s.at[slot, k], c_r.at[slot, k], ctx=xhi * 4 + to).start()
        return carry

    lax.fori_loop(0, 3, weight_block, 0)

    for k in (1, 3, 2):
        arrived(dkr.at[k - 1], dk_r.at[k])

    def over_z(half):
        lanes = pl.ds(pl.multiple_of((half * 4 + z) * CHIP, CHIP), CHIP)
        out = []
        for i in range(2):
            total = acc[i, :, lanes]
            for k in range(3):
                total += dkr[k, half, i].astype(F32)
            out.append(total)
        return out

    for i, total in enumerate(over_z(1 - xhi)):
        dkx[i] = total.astype(BF)
    copy = send(dkx, dkxr, dk_s.at[0], dk_r.at[0], ctx=xctx)
    copy.start()
    sent.append(copy)
    kept = over_z(xhi)
    copy.wait_recv()
    for i in range(2):
        total = (kept[i] + dkxr[i].astype(F32)) * (scale if i == 0 else 1.0)
        gkv[i, core] = total.T.astype(BF)
    gkv_copy = send(gkv.at[:, core], gkv.at[:, core], pair_s.at[4], pair_r.at[4], mod=other)
    gkv_copy.start()
    sent.append(gkv_copy)
    send_grads(gkv.at[0, core], 0, 4, b_s.at[7])
    send_grads(gkv.at[1, core], 1, 3, b_s.at[8])

    for head in range(HEADS):
        arrived(gq.at[:, pl.ds(aligned(other * HEADS + head, HS), HS)], gq_r.at[head])
    arrived(gkv.at[:, other], pair_r.at[4])

    def spread(i, carry):
        rows = pl.ds(aligned(i, 512), 512)
        grads_kv = jnp.concatenate([gkv[0, 0], gkv[0, 1], gkv[1, 0], gkv[1, 1]], axis=1)
        total = dot(gq[...], wq_v[rows, :], ((1,), (1,))) + dot(grads_kv, wkv_v[rows, :], ((1,), (1,)))
        sb[:, rows] = total.astype(BF)
        return carry

    lax.fori_loop(0, 7, spread, 0)
    home_copy = send(sb.at[other_rows], sr, pair_s.at[5], pair_r.at[5], mod=other)
    home_copy.start()
    sent.append(home_copy)

    last = 5 - core
    lax.fori_loop(3, last, weight_block, 0)

    def sum_z(slot, carry):
        for k in (1, 3, 2):
            arrived(crz.at[slot, k - 1], c_r.at[slot, k])
        for e in range(2):
            for half, far in ((1 - xhi, True), (xhi, False)):
                total = cs[slot, z, half, e].astype(F32)
                for k in range(3):
                    total += crz[slot, k, half, e].astype(F32)
                if far:
                    cx[slot, e] = total.astype(BF)
                else:
                    keep[slot, e] = total
        send(cx.at[slot], cxr.at[slot], cx_s.at[slot], cx_r.at[slot], ctx=xctx).start()
        return carry

    lax.fori_loop(0, last, sum_z, 0)
    fin[...] = jnp.zeros_like(fin)

    def sum_x(slot, carry):
        arrived(cxr.at[slot], cx_r.at[slot])
        for e in range(2):
            total = keep[slot, e] + cxr[slot, e].astype(F32)
            for s in range(2):
                padded = jnp.concatenate([total[s * PART:(s + 1) * PART], jnp.zeros((8, HS), F32)], axis=0)
                fin[s, e, slot] = padded.astype(BF)
        return carry

    lax.fori_loop(0, last, sum_x, 0)
    for s in range(2):
        for e in range(2):
            at_home = jnp.logical_and(xlo == s, core == e)
            copy = send(
                fin.at[s, e], finr.at[xlo, core], fin_s.at[s, e], fin_r.at[xlo, core], dp=s * 4 + y, mod=e
            )

            @pl.when(at_home)
            def _():
                pltpu.make_async_copy(fin.at[s, e], finr.at[xlo, core], fin_r.at[xlo, core]).start()

            @pl.when(jnp.logical_not(at_home))
            def _():
                copy.start()

    for head in range(HEADS):
        lanes = pl.ds(aligned(other * HEADS + head, HS), HS)
        arrived(attf.at[:, lanes], att_r.at[head])
    att_o[...] = attf[...]
    arrived(sr, pair_r.at[5])
    pick = jnp.broadcast_to(mods[here][0:1, 0:1], (BLOCK, D)) == expert
    gh_o[...] = jnp.where(pick, sb[own_rows, :], sr[...])

    for g in range(2):
        for c in range(2):
            arrived(finr.at[g, c], fin_r.at[g, c])
    for g in range(2):
        for head in range(HEADS):
            cols = slice((g * HEADS + head) * HS, (g * HEADS + head + 1) * HS)
            gwq_o[:, cols] = finr[g, head // 4, head % 4][:PART]
        gwkv_o[:, g * HS:(g + 1) * HS] = finr[g, 0, 4][:PART]
        gwkv_o[:, KW + g * HS:KW + (g + 1) * HS] = finr[g, 1, 3][:PART]

    for copy in sent:
        copy.wait_send()

    def heads_sent(head, carry):
        full_lanes = pl.ds(aligned(core * HEADS + head, HS), HS)
        send(
            attb.at[head, other_rows], attf.at[:, full_lanes], att_s.at[head], att_r.at[head], mod=other
        ).wait_send()
        send(dqb.at[head], gq.at[:, full_lanes], gq_s.at[head], gq_r.at[head], mod=other).wait_send()
        grads_sent(dqb.at[head], head // 4, head % 4, b_s.at[head])
        return carry

    lax.fori_loop(0, HEADS, heads_sent, 0)
    grads_sent(gkv.at[0, core], 0, 4, b_s.at[7])
    grads_sent(gkv.at[1, core], 1, 3, b_s.at[8])

    def blocks_sent(slot, carry):
        for k in (1, 3, 2):
            to = (z + k) % 4
            send(cs.at[slot, to], crz.at[slot, k - 1], c_s.at[slot, k], c_r.at[slot, k], ctx=xhi * 4 + to).wait_send()
        send(cx.at[slot], cxr.at[slot], cx_s.at[slot], cx_r.at[slot], ctx=xctx).wait_send()
        return carry

    lax.fori_loop(0, last, blocks_sent, 0)
    for s in range(2):
        for e in range(2):
            copy = send(
                fin.at[s, e], finr.at[xlo, core], fin_s.at[s, e], fin_r.at[xlo, core], dp=s * 4 + y, mod=e
            )

            @pl.when(jnp.logical_not(jnp.logical_and(xlo == s, core == e)))
            def _():
                copy.wait_send()


def on_device(hidden_in, out_grad, modality, segment, w_query, w_keyval):
    vmem, dma = pltpu.VMEM, pltpu.SemaphoreType.DMA
    scratch = [
        vmem((D, QW), BF), vmem((D, 2 * KW), BF),
        vmem((CHIP, D), BF), vmem((D, BLOCK), BF), vmem((CHIP, GW), BF), vmem((16, 8, HS), F32),
        vmem((2 * SLICE, SEQ), BF),
        vmem((2, 2, CHIP, HS), BF), vmem((2, CHIP, HS), BF), vmem((2, SEQ, HS), BF),
        vmem((2, CHIP, GW), BF), vmem((CHIP, GW), BF), vmem((CHIP, GW), BF), vmem((CHIP, SEQ), F32),
        vmem((HEADS, CHIP, HS), BF), vmem((BLOCK, QW), BF), vmem((HEADS, CHIP, HS), BF), vmem((CHIP, QW), BF),
        vmem((2, HS, SEQ), F32), vmem((2, 4, 2, HS, CHIP), BF), vmem((3, 2, 2, HS, CHIP), BF),
        vmem((2, HS, CHIP), BF), vmem((2, HS, CHIP), BF), vmem((2, 2, CHIP, HS), BF),
        vmem((5, SEQ, HS), BF), vmem((SEQ, 2 * HS), BF), vmem((2 * SLICE, 2 * HS), F32),
        vmem((5, 4, 2, 2, 2 * PART, HS), BF), vmem((5, 3, 2, 2, 2 * PART, HS), BF),
        vmem((5, 2, 2 * PART, HS), BF), vmem((5, 2, 2 * PART, HS), BF), vmem((5, 2, 2 * PART, HS), F32),
        vmem((2, 2, 5, 64, HS), BF), vmem((2, 2, 5, 64, HS), BF),
        vmem((CHIP, D), BF), vmem((BLOCK, D), BF),
        dma((5,)), dma((6,)), dma((6,)), dma((8, 2)), dma((8, 2)), dma((8, 2)), dma((8, 2)), dma((8,)), dma((8,)),
        dma((2, 4)), dma((2, 4)), dma((HEADS,)), dma((HEADS,)), dma((HEADS,)), dma((HEADS,)),
        dma((9, 4)), dma((5, 8)), dma((4,)), dma((4,)), dma((5, 4)), dma((5, 4)), dma((5,)), dma((5,)),
        dma((2, 2)), dma((2, 2)),
    ]
    in_vmem, anywhere = pl.BlockSpec(memory_space=pltpu.VMEM), pl.BlockSpec(memory_space=pl.ANY)
    kinds = jnp.broadcast_to(modality.astype(F32), (8, BLOCK))
    segs = jnp.broadcast_to(segment.astype(F32), (8, SEQ))
    attended, grad_hidden, grad_wq, grad_wkv = pl.pallas_call(
        layer,
        out_shape=(
            jax.ShapeDtypeStruct((BLOCK, QW), BF),
            jax.ShapeDtypeStruct((BLOCK, D), BF),
            jax.ShapeDtypeStruct((PART, QW), BF),
            jax.ShapeDtypeStruct((PART, 2 * KW), BF),
        ),
        in_specs=[in_vmem] * 4 + [anywhere] * 2,
        out_specs=(in_vmem,) * 4,
        scratch_shapes=scratch,
        compiler_params=pltpu.CompilerParams(
            collective_id=0, has_side_effects=True, vmem_limit_bytes=63 * 2**20
        ),
        name="layer",
    )(hidden_in[0], out_grad[0], kinds, segs, w_query[0], w_keyval[0])
    return attended[None], grad_hidden[None], grad_wq[None], grad_wkv[None]


def solution(mesh):
    return jax.shard_map(
        on_device,
        mesh=mesh,
        in_specs=(
            P("dp", ("ctx", "mod"), None),
            P("dp", ("ctx", "mod"), None),
            P("dp", ("ctx", "mod")),
            P("dp", None),
            P("mod", None, None),
            P("mod", None, None),
        ),
        out_specs=(
            P("dp", ("ctx", "mod"), None),
            P("dp", ("ctx", "mod"), None),
            P("mod", ("dp", "ctx"), None),
            P("mod", ("dp", "ctx"), None),
        ),
        check_vma=False,
    )
```

time: 524 us -> 120 us (0.23)
  waiting for transfers between devices: 339 us -> 0 us
  Pallas kernels: 0 us -> 108 us
  matrix products: 99.4 us -> 0 us
  blocking collectives: 18.8 us -> 0 us
  local copies, waits for them, and re-layouts: 26.4 us -> 8.27 us
  other arithmetic: 19.3 us -> 1.36 us
  between operations: 14.1 us -> 0.64 us
    reduce_scatter x3 -> x0, waiting for transfers between devices: 290 us -> none  [the longest x1 168 us: on_device(): lax.psum_scatter(partial_sum.astype(jnp.bfloat16), 'dp', scatter_dimensio...]
    pallas_call x0 -> x1, Pallas kernels: none -> 108 us  [on_device(): pl.pallas_call(layer, out_shape=(jax.ShapeDtypeStruct((BLOCK, QW), BF), j...]
    dot_general x31 -> x0, matrix products: 99.4 us -> none  [the longest x8 27.1 us: score_block(): jnp.einsum('rgjd,ngd->gjrn', queries, key_rows, preferred_element_type=jn...]
    all_gather x1 -> x0, waiting for transfers between devices: 47.7 us -> none  [on_device(): lax.all_gather(projected[:, query_width:], ('ctx', 'mod'), axis=0, tiled=...]
    all_to_all x3 -> x0, blocking collectives: 18.8 us -> none  [the longest x1 6.88 us: on_device(): lax.all_to_all(grad_packed, 'mod', split_axis=0, concat_axis=0, tiled=True)]
    reduce_sum x4 -> x0, other arithmetic: 11.1 us -> none  [forward_step(): weight_sum = weight_sum * fade + jnp.sum(weights, axis=-1)]
    unnamed x16 -> x4, local copies, waits for them, and re-layouts: 12.7 us -> 7.04 us
  transfers between devices with their start and end apart: 5 -> 0, of which waited for: 5 -> 0; matrix products, arithmetic and copies ran while one was open for 3% -> 0% of each run, Pallas kernels for 0% -> 0%
where the time goes in v1:
time: 120 us; the launch traced here: 119 us
  Pallas kernels  108 us (90%)
  local copies, waits for them, and re-layouts  8.27 us (7%)
  other arithmetic  1.36 us (1%)
    pallas_call x1, Pallas kernels, on_device(): pl.pallas_call(layer, out_shape=(jax.ShapeDtypeStruct((BLOCK, QW), BF), j...  108 us
    unnamed x4, local copies, waits for them, and re-layouts  7.04 us

profile of v1, /device:TPU:1, one launch (start us, length us, event | category | flops | bytes accessed | tf_op | source)
XLA Modules:
  0.0 118.5 jit_solution(4165794114338968988)
XLA Ops:
  0.6 0.7 convert_bitcast_fusion
  1.3 0.6 broadcast_in_dim.27.modv
  1.9 0.7 convert_element_type.7
  2.6 0.6 broadcast_in_dim.29.segv
  3.2 108.3 %layer.1 = (bf16[128,1792]{1,0:T(8,128)(2,1)}, bf16[128,3584]{1,0:T(8,128)(2,1)}, bf16[56,1792]{1,0:T(8,128)(2,1)}, bf16[56,512]{1,0:T(8,128)(2,1)}) custom-call(bf16[128,3584]{1,0:T(8,128)(2,1)} %bitcast.14, bf16[128,1792]{1,0:T(8,128)(2,1)} %bitcast.16, f32[8,128]{1,0:T(8,128)} %broadcast_in_dim.27.modv, f32[8,2048]{1,0:T(8,128)} %broadcast_in_dim.29.segv, ...), custom_call_target="tpu_custom_call" | custom-call | tf_op jit(solution)/shard_map/layer/pallas_call | solution.py:473
  111.5 1.8 %copy.14 = bf16[1,128,1792]{2,1,0:T(8,128)(2,1)} copy(bf16[1,128,1792]{2,1,0:T(8,128)(2,1)} %bitcast.15) | data formatting | bytes 917504
  113.3 2.2 %copy.15 = bf16[1,128,3584]{2,1,0:T(8,128)(2,1)} copy(bf16[1,128,3584]{2,1,0:T(8,128)(2,1)} %bitcast.13) | data formatting | bytes 1835008
  115.5 1.6 %copy.16 = bf16[1,56,1792]{2,1,0:T(8,128)(2,1)} copy(bf16[1,56,1792]{2,1,0:T(8,128)(2,1)} %bitcast.17) | data formatting | bytes 401408
  117.1 1.4 %copy.17 = bf16[1,56,512]{2,1,0:T(8,128)(2,1)} copy(bf16[1,56,512]{2,1,0:T(8,128)(2,1)} %bitcast.18) | data formatting | bytes 114688

commit v2 on v1

v2 whole, which is shorter than its diff:
```python
import functools
import math

import jax
import jax.numpy as jnp
from jax import lax
from jax.experimental import pallas as pl
from jax.experimental.pallas import tpu as pltpu
from jax.sharding import PartitionSpec as P

HS = 128
BLOCK = 128
D = 3584
QW = 1792
KW = 256
SEQ = 2048
HEADS = 7
GW = HEADS * HS
CHIP = 2 * BLOCK
SLICE = 448
PART = 56
LAG = 2
MESH = pl.DeviceIdType.MESH
BF = jnp.bfloat16
F32 = jnp.float32


def aligned(index, step):
    return pl.multiple_of(index * step, step)


def dot(a, b, dims=((1,), (0,))):
    return lax.dot_general(a, b, (dims, ((), ())), preferred_element_type=F32)


def send(src, dst, send_sem, recv_sem, **device):
    return pltpu.make_async_remote_copy(
        src_ref=src, dst_ref=dst, send_sem=send_sem, recv_sem=recv_sem,
        device_id=device, device_id_type=MESH,
    )


def arrived(dst, sem):
    pltpu.make_async_copy(dst, dst, sem).wait()


def layer(
    hid_h, og_h, kinds, segs, wq, wkv,
    attf, gh_o, finr,
    hid, og, wq_v, wkv_v, hidf, hid_t, ogf, mods, at, kvs, kvr, kvall, qs, qr, qf, bias,
    modv, attb, dqb, dqx, gq, acc, dkvb, dkr, dvr, dvz, dvzr, dkx, dkxr, gkv, gkvx, bg, be, cf, cs, cs1, crz, crx, cx, cxr, cz, czr, keep, fin, sb, sr,
    w_sem, pair_s, pair_r, mod_s, mod_r, a_s, a_r, af_s, af_r, kv_s, kv_r,
    att_s, att_r, gq_s, gq_r, bx_s, bx_r, b_s, b_r, dk_s, dk_r, c_s, c_r, cx_s, cx_r, fin_s, fin_r,
):
    dp, ctx, core = lax.axis_index("dp"), lax.axis_index("ctx"), lax.axis_index("mod")
    xlo, y, xhi, z = dp // 4, dp % 4, ctx // 4, ctx % 4
    other = 1 - core
    here = dp * 2 + core
    expert = core.astype(F32)
    scale = 1.0 / math.sqrt(HS)

    q_cols = []
    for group in (other, core):
        for first, width in ((0, 512), (512, 384)):
            q_cols.append((group, first, width))
    own_loads = [
        pltpu.make_async_copy(hid_h, hid, w_sem.at[5]), pltpu.make_async_copy(og_h, og, w_sem.at[6])
    ]
    loads = [pltpu.make_async_copy(wkv, wkv_v, w_sem.at[0])]
    for i, (group, first, width) in enumerate(q_cols):
        cols = pl.ds(pl.multiple_of(group * GW + first, 128), width)
        loads.append(pltpu.make_async_copy(wq.at[:, cols], wq_v.at[:, cols], w_sem.at[1 + i]))
    barrier = pltpu.get_barrier_semaphore()
    for k in range(8):
        pl.semaphore_signal(barrier, inc=1, device_id={"dp": (dp + k) % 8, "mod": other}, device_id_type=MESH)
        if k:
            pl.semaphore_signal(barrier, inc=1, device_id={"dp": (dp + k) % 8}, device_id_type=MESH)
            pl.semaphore_signal(barrier, inc=1, device_id={"ctx": (ctx + k) % 8}, device_id_type=MESH)
    for load in own_loads + loads:
        load.start()
    for load in own_loads:
        load.wait()
    pl.semaphore_wait(barrier, 22)

    own_rows = pl.ds(aligned(core, BLOCK), BLOCK)
    other_rows = pl.ds(aligned(other, BLOCK), BLOCK)
    sent = []

    hid_copy = send(hid, hidf.at[own_rows], pair_s.at[0], pair_r.at[0], mod=other)
    hid_copy.start()
    og_copy = send(og.at[:, pl.ds(aligned(other, GW), GW)], ogf.at[own_rows], pair_s.at[1], pair_r.at[1], mod=other)
    og_copy.start()
    sent += [hid_copy, og_copy]
    modv[...] = jnp.broadcast_to(kinds[...].astype(F32), (8, BLOCK))
    mods[here] = modv[...]
    for k in range(8):
        for c in range(2):
            if k == 0 and c == 0:
                continue
            dev = {"dp": (dp + k) % 8, "mod": other if c else core}
            copy = send(modv, mods.at[here], mod_s.at[k, c], mod_r.at[k, c], **dev)
            copy.start()
            sent.append(copy)
    hidf[own_rows, :] = hid[...]
    ogf[own_rows, :] = og[:, pl.ds(aligned(core, GW), GW)]

    here_lanes = pl.ds(aligned(here, BLOCK), BLOCK)
    for i in range(7):
        hid_t[i * 512:(i + 1) * 512, :] = hid[:, i * 512:(i + 1) * 512].T
    def send_hidden(side, k):
        to = (y + k) % 4
        for s in range(2):
            rows = pl.ds(pl.multiple_of((s * 4 + to) * SLICE, 64), SLICE)
            copy = send(
                hid_t.at[rows], at.at[pl.ds(s * SLICE, SLICE), here_lanes], a_s.at[side, k, s], a_r.at[side, k, s],
                dp=(xlo if side == 0 else 1 - xlo) * 4 + to,
            )
            copy.start()
            sent.append(copy)

    for side, k in ((1, 0), (0, 1), (0, 3), (0, 2)):
        send_hidden(side, k)
    for s in range(2):
        rows = pl.ds(pl.multiple_of((s * 4 + y) * SLICE, 64), SLICE)
        at[s * SLICE:(s + 1) * SLICE, here_lanes] = hid_t[rows, :]

    def lanes_of(side, k):
        return pl.ds(pl.multiple_of((((xlo if side == 0 else 1 - xlo) * 4 + (y - k + 4) % 4) * 2 + core) * BLOCK, BLOCK), BLOCK)

    def pass_hidden(side, k):
        lanes = lanes_of(side, k)
        return send(at.at[:, lanes], at.at[:, lanes], af_s.at[side, k], af_r.at[side, k], mod=other)

    def relay_hidden(side, k):
        if side or k:
            for s in range(2):
                arrived(at.at[pl.ds(s * SLICE, SLICE), lanes_of(side, k)], a_r.at[side, k, s])
        pass_hidden(side, k).start()

    hid_copy.wait_recv()
    loads[0].wait()
    made = dot(hidf[...], wkv_v[...]).astype(BF)
    for i in range(2):
        for g in range(2):
            kvs[i, g] = made[:, (i * 2 + g) * HS:(i * 2 + g + 1) * HS]
    copy = send(kvs.at[:, other], kvr, pair_s.at[2], pair_r.at[2], mod=other)
    copy.start()
    sent.append(copy)
    def other_kinds():
        for k in range(1, 8):
            for c in range(2):
                arrived(mods.at[(dp - k + 8) % 8 * 2 + (other if c else core)], mod_r.at[k, c])
    arrived(mods.at[dp * 2 + other], mod_r.at[0, 1])
    mine = [
        jnp.broadcast_to(mods[dp * 2 + b][0:1, :], (BLOCK, HS)) == expert for b in range(2)
    ]
    copy.wait_recv()
    for i in range(2):
        for b in range(2):
            rows = slice(b * BLOCK, (b + 1) * BLOCK)
            kvall[i, pl.ds(pl.multiple_of(ctx * CHIP + b * BLOCK, BLOCK), BLOCK), :] = jnp.where(
                mine[b], kvs[i, core, rows, :], kvr[i, rows, :]
            )
    ctx_rows = pl.ds(aligned(ctx, CHIP), CHIP)
    xctx = (1 - xhi) * 4 + z
    xctx_rows = pl.ds(aligned(xctx, CHIP), CHIP)

    def rows_from(side, k):
        return pl.ds(aligned((xhi if side == 0 else 1 - xhi) * 4 + (z - k + 4) % 4, CHIP), CHIP)

    def send_keys(i, side, k, rows, to):
        copy = send(kvall.at[i, rows], kvall.at[i, rows], kv_s.at[i, side, k], kv_r.at[i, side, k], ctx=to)
        copy.start()
        sent.append(copy)

    def keys_from(i, side, k):
        arrived(kvall.at[i, rows_from(side, k)], kv_r.at[i, side, k])

    for i in range(2):
        send_keys(i, 1, 0, ctx_rows, xctx)
    for k in (1, 3, 2):
        for i in range(2):
            send_keys(i, 0, k, ctx_rows, xhi * 4 + (z + k) % 4)

    def project(i):
        group, first, width = q_cols[i]
        loads[1 + i].wait()
        cols = pl.ds(pl.multiple_of(group * GW + first, 128), width)
        qs[group, :, first:first + width] = dot(hidf[...], wq_v[:, cols]).astype(BF)

    project(0)
    for i in range(2):
        keys_from(i, 1, 0)
        for k in (1, 3, 2):
            send_keys(i, 1, k, xctx_rows, xhi * 4 + (z + k) % 4)
    for k in (2, 1, 3):
        send_hidden(1, k)
    project(1)
    q_copy = send(qs.at[other], qr, pair_s.at[3], pair_r.at[3], mod=other)
    q_copy.start()
    sent.append(q_copy)
    project(2)
    project(3)
    seg_rows = segs[:, pl.ds(aligned(ctx, CHIP), CHIP)].astype(F32)
    seg_col = jnp.broadcast_to(seg_rows, (128, CHIP)).T[:, 0:1]
    bias[...] = jnp.where(segs[...].astype(F32) <= seg_col, 0.0, -1e30)
    acc[...] = jnp.zeros_like(acc)
    q_copy.wait_recv()
    for b in range(2):
        rows = slice(b * BLOCK, (b + 1) * BLOCK)
        pick = jnp.broadcast_to(mods[dp * 2 + b][0:1, 0:1], (BLOCK, GW)) == expert
        qf[rows, :] = jnp.where(pick, qs[core, rows, :], qr[rows, :])
    og_copy.wait_recv()
    for i in range(2):
        for k in (1, 3, 2):
            keys_from(i, 0, k)
            keys_from(i, 1, k)

    def one_head(i, carry):
        slot, target = i // 2, i % 2
        head = target * 4 + slot
        lanes = pl.ds(aligned(head, HS), HS)
        full_lanes = pl.ds(aligned(core * HEADS + head, HS), HS)
        q, go = qf[:, lanes], ogf[:, lanes]
        keys, values = kvall[0], kvall[1]
        scores = dot(q, keys, ((1,), (1,))) * (scale * math.log2(math.e)) + bias[...]
        top = jnp.max(scores, axis=1, keepdims=True)
        weights = jnp.exp2(scores - top)
        total = jnp.sum(weights, axis=1, keepdims=True)
        low = weights.astype(BF)
        inv = 1.0 / total
        attended = (dot(low, values) * inv).astype(BF)
        attb[head] = attended
        copy = send(
            attb.at[head, other_rows], attf.at[:, full_lanes], att_s.at[head], att_r.at[head], mod=other
        )
        copy.start()
        attf[:, full_lanes] = attb[head, own_rows, :]
        go32 = go.astype(F32)
        delta = jnp.sum(go32 * attended.astype(F32), axis=1, keepdims=True)
        dprob = dot(go, values, ((1,), (1,)))
        dscore = (weights * (dprob * inv - delta * inv)).astype(BF)
        dq = (dot(dscore, keys) * scale).astype(BF)
        dqb[head] = dq
        gq[:, full_lanes] = dq
        copy = send(dqb.at[head], gq.at[:, full_lanes], gq_s.at[head], gq_r.at[head], mod=other)
        copy.start()
        spread_grads(i, head, target, slot)
        acc[0] += dot(q.T, dscore)
        acc[1] += dot((go32 * inv).astype(BF).T, low)

        @pl.when(i == 2)
        def _():
            for k in (0, 1, 3, 2):
                relay_hidden(0, k)

        @pl.when(i == 4)
        def _():
            for k in (0, 2, 1, 3):
                relay_hidden(1, k)

        return carry

    home = xlo == core

    def cross(head):
        return send(dqb.at[head], dqx.at[head], bx_s.at[head], bx_r.at[head], dp=(1 - xlo) * 4 + y)

    def cross_kv():
        return send(gkv.at[:, core], gkvx, bx_s.at[HEADS], bx_r.at[HEADS], dp=(1 - xlo) * 4 + y)

    def fan(src, side, target, slot, sems, k):
        rows = pl.ds(pl.multiple_of((side * 4 + y) * CHIP, CHIP), CHIP)
        return send(
            src, bg.at[slot, rows], sems.at[k], b_r.at[slot, side * 4 + y], dp=xlo * 4 + (y + k) % 4, mod=target
        )

    def fan_out(src, side, target, slot, sems):
        rows = pl.ds(pl.multiple_of((side * 4 + y) * CHIP, CHIP), CHIP)
        for k in (1, 3, 2):
            fan(src, side, target, slot, sems, k).start()

        @pl.when(target == core)
        def _():
            pltpu.make_async_copy(src, bg.at[slot, rows], b_r.at[slot, side * 4 + y]).start()

        @pl.when(target != core)
        def _():
            fan(src, side, target, slot, sems, 0).start()

    def fan_sent(src, side, target, slot, sems):
        for k in (1, 3, 2):
            fan(src, side, target, slot, sems, k).wait_send()

        @pl.when(target != core)
        def _():
            fan(src, side, target, slot, sems, 0).wait_send()

    def relay_grads(i):
        slot, target = i // 2, i % 2
        head = target * 4 + slot
        arrived(dqx.at[head], bx_r.at[head])
        fan_out(dqx.at[head], 1 - xlo, target, slot, b_s.at[1, head])

    def spread_grads(i, head, target, slot):
        @pl.when(jnp.logical_not(home))
        def _():
            cross(head).start()

        @pl.when(home)
        def _():
            fan_out(dqb.at[head], xlo, target, slot, b_s.at[0, head])

            @pl.when(i >= LAG)
            def _():
                relay_grads(i - LAG)

    def block_sums(slot):
        for source in range(8):
            arrived(bg.at[slot, pl.ds(source * CHIP, CHIP)], b_r.at[slot, source])
        for t in range(16):
            rows = slice(t * BLOCK, (t + 1) * BLOCK)
            kind = mods[t][0:1, :]
            block = bg[slot, rows, :]
            second = jnp.where(jnp.broadcast_to(kind, (BLOCK, HS)) == 1.0, block, jnp.zeros_like(block))
            be[rows, HS:] = second
            be[rows, :HS] = block - second
        cf[...] = dot(at[...], be[...])
        for c in range(8):
            for e, buf in enumerate((cs, cs1)):
                cols = slice(e * HS, (e + 1) * HS)
                both = jnp.concatenate(
                    [cf[c * PART:(c + 1) * PART, cols], cf[SLICE + c * PART:SLICE + (c + 1) * PART, cols]], axis=0
                )
                buf[slot, c % 4, c // 4] = both.astype(BF)

    def z_leg(slot, k):
        to = (z + k) % 4
        return send(cs.at[slot, to], crz.at[slot, k - 1], c_s.at[slot, k], c_r.at[slot, k], ctx=xhi * 4 + to)

    def x_leg(slot):
        return send(cs1.at[slot, :, 1 - xhi], crx.at[slot], c_s.at[slot, 0], c_r.at[slot, 0], ctx=xctx)

    def then_x(slot):
        return send(cx.at[slot], cxr.at[slot], cx_s.at[slot, 0], cx_r.at[slot, 0], ctx=xctx)

    def then_z(slot, k):
        to = (z + k) % 4
        return send(cz.at[slot, to], czr.at[slot, k - 1], cx_s.at[slot, k], cx_r.at[slot, k], ctx=xhi * 4 + to)

    def z_legs(slot):
        for k in (1, 3, 2):
            z_leg(slot, k).start()

    def x_legs(slot):
        x_leg(slot).start()

    def first_leg(slot):
        x_legs(slot)
        z_legs(slot)

    def second_leg(slot):
        arrived(crx.at[slot], c_r.at[slot, 0])
        for k in (1, 3, 2):
            to = (z + k) % 4
            cz[slot, to] = (cs1[slot, to, xhi].astype(F32) + crx[slot, to].astype(F32)).astype(BF)
            then_z(slot, k).start()
        keep[slot, 1] = cs1[slot, z, xhi].astype(F32) + crx[slot, z].astype(F32)
        for k in (1, 3, 2):
            arrived(crz.at[slot, k - 1], c_r.at[slot, k])
        total = cs[slot, z, 1 - xhi].astype(F32)
        for k in range(3):
            total += crz[slot, k, 1 - xhi].astype(F32)
        cx[slot] = total.astype(BF)
        then_x(slot).start()
        total = cs[slot, z, xhi].astype(F32)
        for k in range(3):
            total += crz[slot, k, xhi].astype(F32)
        keep[slot, 0] = total

    def last_leg(slot):
        for k in (1, 3, 2):
            arrived(czr.at[slot, k - 1], cx_r.at[slot, k])
        arrived(cxr.at[slot], cx_r.at[slot, 0])
        second = keep[slot, 1]
        for k in range(3):
            second += czr[slot, k].astype(F32)
        for e, total in enumerate((keep[slot, 0] + cxr[slot].astype(F32), second)):
            for s in range(2):
                padded = jnp.concatenate([total[s * PART:(s + 1) * PART], jnp.zeros((8, HS), F32)], axis=0)
                fin[s, e, slot] = padded.astype(BF)

    def each(step):
        def run(slot, carry):
            step(slot)
            return carry

        return run

    lax.fori_loop(0, HEADS, one_head, 0)

    @pl.when(home)
    def _():
        for i in range(HEADS - LAG, HEADS):
            relay_grads(i)

    for c in range(8):
        for i in range(2):
            dkvb[i, c // 4, c % 4] = acc[i, :, c * CHIP:(c + 1) * CHIP].astype(BF)
    copies = [send(dkvb.at[1, 1 - xhi], dvr, dk_s.at[0], dk_r.at[0], ctx=xctx)]
    for k in (1, 3, 2):
        to = (z + k) % 4
        copies.append(send(dkvb.at[0, :, to], dkr.at[k - 1], dk_s.at[k], dk_r.at[k], ctx=xhi * 4 + to))
    for copy in copies:
        copy.start()
        sent.append(copy)

    last = 5 - core
    for side in range(2):
        for k in range(4):
            lanes = pl.ds(
                pl.multiple_of((((xlo if side == 0 else 1 - xlo) * 4 + (y - k + 4) % 4) * 2 + other) * BLOCK, BLOCK),
                BLOCK,
            )
            arrived(at.at[:, lanes], af_r.at[side, k])
    other_kinds()
    lax.fori_loop(0, 2, each(block_sums), 0)
    for head in range(HEADS):
        arrived(gq.at[:, pl.ds(aligned(other * HEADS + head, HS), HS)], gq_r.at[head])

    def spread(i, carry):
        rows = pl.ds(aligned(i, 512), 512)
        total = dot(gq[...], wq_v[rows, :], ((1,), (1,)))
        high = total.astype(BF)
        hidf[:, rows] = high
        sb[:, rows] = (total - high.astype(F32)).astype(BF)
        return carry

    lax.fori_loop(0, 7, spread, 0)

    copies[0].wait_recv()
    for k in (1, 3, 2):
        to = (z + k) % 4
        lanes = pl.ds(pl.multiple_of((xhi * 4 + to) * CHIP, CHIP), CHIP)
        dvz[to] = (acc[1, :, lanes] + dvr[to].astype(F32)).astype(BF)
        copy = send(dvz.at[to], dvzr.at[k - 1], dk_s.at[4 + k], dk_r.at[4 + k], ctx=xhi * 4 + to)
        copy.start()
        sent.append(copy)
    for k in (1, 3, 2):
        arrived(dkr.at[k - 1], dk_r.at[k])

    def over_z(half):
        total = acc[0, :, pl.ds(pl.multiple_of((half * 4 + z) * CHIP, CHIP), CHIP)]
        for k in range(3):
            total += dkr[k, half].astype(F32)
        return total

    dkx[...] = over_z(1 - xhi).astype(BF)
    dk_copy = send(dkx, dkxr, dk_s.at[4], dk_r.at[4], ctx=xctx)
    dk_copy.start()
    sent.append(dk_copy)
    lax.fori_loop(0, 2, each(first_leg), 0)
    lax.fori_loop(2, last - 1, each(block_sums), 0)
    dk = over_z(xhi)
    dv = acc[1, :, pl.ds(pl.multiple_of((xhi * 4 + z) * CHIP, CHIP), CHIP)] + dvr[z].astype(F32)
    for k in (1, 3, 2):
        arrived(dvzr.at[k - 1], dk_r.at[4 + k])
    for k in range(3):
        dv += dvzr[k].astype(F32)
    gkv[1, core] = dv.T.astype(BF)
    dk_copy.wait_recv()
    dk = (dk + dkxr[...].astype(F32)) * scale
    gkv[0, core] = dk.T.astype(BF)
    gkv_copy = send(gkv.at[:, core], gkv.at[:, core], pair_s.at[4], pair_r.at[4], mod=other)
    gkv_copy.start()
    sent.append(gkv_copy)

    @pl.when(jnp.logical_not(home))
    def _():
        cross_kv().start()

    @pl.when(home)
    def _():
        for i, target, slot in ((0, 0, 4), (1, 1, 3)):
            fan_out(gkv.at[i, core], xlo, target, slot, b_s.at[0, HEADS + i])

    lax.fori_loop(2, last - 1, each(first_leg), 0)
    lax.fori_loop(0, 2, each(second_leg), 0)

    @pl.when(home)
    def _():
        arrived(gkvx, bx_r.at[HEADS])
        for i, target, slot in ((0, 0, 4), (1, 1, 3)):
            fan_out(gkvx.at[i], 1 - xlo, target, slot, b_s.at[1, HEADS + i])

    arrived(gkv.at[:, other], pair_r.at[4])
    grads_kv = jnp.concatenate([gkv[0, 0], gkv[0, 1], gkv[1, 0], gkv[1, 1]], axis=1)
    for i in range(7):
        rows = slice(i * 512, (i + 1) * 512)
        total = hidf[:, rows].astype(F32) + sb[:, rows].astype(F32) + dot(grads_kv, wkv_v[rows, :], ((1,), (1,)))
        sb[:, rows] = total.astype(BF)
    home_copy = send(sb.at[other_rows], sr, pair_s.at[5], pair_r.at[5], mod=other)
    home_copy.start()
    sent.append(home_copy)

    block_sums(last - 1)
    first_leg(last - 1)

    fin[...] = jnp.zeros_like(fin)
    lax.fori_loop(2, last, each(second_leg), 0)
    lax.fori_loop(0, last, each(last_leg), 0)
    for s in range(2):
        for e in range(2):
            at_home = jnp.logical_and(xlo == s, core == e)
            copy = send(
                fin.at[s, e], finr.at[xlo, core], fin_s.at[s, e], fin_r.at[xlo, core], dp=s * 4 + y, mod=e
            )

            @pl.when(at_home)
            def _():
                pltpu.make_async_copy(fin.at[s, e], finr.at[xlo, core], fin_r.at[xlo, core]).start()

            @pl.when(jnp.logical_not(at_home))
            def _():
                copy.start()

    for head in range(HEADS):
        lanes = pl.ds(aligned(other * HEADS + head, HS), HS)
        arrived(attf.at[:, lanes], att_r.at[head])
    arrived(sr, pair_r.at[5])
    pick = jnp.broadcast_to(mods[here][0:1, 0:1], (BLOCK, D)) == expert
    gh_o[...] = jnp.where(pick, sb[own_rows, :], sr[...])

    for g in range(2):
        for c in range(2):
            arrived(finr.at[g, c], fin_r.at[g, c])

    for copy in sent:
        copy.wait_send()

    def heads_sent(head, carry):
        full_lanes = pl.ds(aligned(core * HEADS + head, HS), HS)
        send(
            attb.at[head, other_rows], attf.at[:, full_lanes], att_s.at[head], att_r.at[head], mod=other
        ).wait_send()
        send(dqb.at[head], gq.at[:, full_lanes], gq_s.at[head], gq_r.at[head], mod=other).wait_send()

        @pl.when(jnp.logical_not(home))
        def _():
            cross(head).wait_send()

        @pl.when(home)
        def _():
            fan_sent(dqb.at[head], xlo, head // 4, head % 4, b_s.at[0, head])
            fan_sent(dqx.at[head], 1 - xlo, head // 4, head % 4, b_s.at[1, head])

        return carry

    lax.fori_loop(0, HEADS, heads_sent, 0)
    for side in range(2):
        for k in range(4):
            pass_hidden(side, k).wait_send()

    @pl.when(jnp.logical_not(home))
    def _():
        cross_kv().wait_send()

    @pl.when(home)
    def _():
        for i, target, slot in ((0, 0, 4), (1, 1, 3)):
            fan_sent(gkv.at[i, core], xlo, target, slot, b_s.at[0, HEADS + i])
            fan_sent(gkvx.at[i], 1 - xlo, target, slot, b_s.at[1, HEADS + i])

    def blocks_sent(slot, carry):
        x_leg(slot).wait_send()
        then_x(slot).wait_send()
        for k in (1, 3, 2):
            z_leg(slot, k).wait_send()
            then_z(slot, k).wait_send()
        return carry

    lax.fori_loop(0, last, blocks_sent, 0)
    for s in range(2):
        for e in range(2):
            copy = send(
                fin.at[s, e], finr.at[xlo, core], fin_s.at[s, e], fin_r.at[xlo, core], dp=s * 4 + y, mod=e
            )

            @pl.when(jnp.logical_not(jnp.logical_and(xlo == s, core == e)))
            def _():
                copy.wait_send()


def results(att, gh, fin, att_o, gh_o, gwq_o, gwkv_o):
    att_o[...] = att[...]
    gh_o[...] = gh[...]
    for g in range(2):
        for head in range(HEADS):
            cols = slice((g * HEADS + head) * HS, (g * HEADS + head + 1) * HS)
            gwq_o[:, cols] = fin[g, head // 4, head % 4][:PART]
        gwkv_o[:, g * HS:(g + 1) * HS] = fin[g, 0, 4][:PART]
        gwkv_o[:, KW + g * HS:KW + (g + 1) * HS] = fin[g, 1, 3][:PART]


def on_device(hidden_in, out_grad, modality, segment, w_query, w_keyval):
    vmem, dma = pltpu.VMEM, pltpu.SemaphoreType.DMA
    scratch = [
        vmem((BLOCK, D), BF), vmem((BLOCK, QW), BF), vmem((D, QW), BF), vmem((D, 2 * KW), BF),
        vmem((CHIP, D), BF), vmem((D, BLOCK), BF), vmem((CHIP, GW), BF), vmem((16, 8, HS), F32),
        vmem((2 * SLICE, SEQ), BF),
        vmem((2, 2, CHIP, HS), BF), vmem((2, CHIP, HS), BF), vmem((2, SEQ, HS), BF),
        vmem((2, CHIP, GW), BF), vmem((CHIP, GW), BF), vmem((CHIP, GW), BF), vmem((CHIP, SEQ), F32),
        vmem((8, BLOCK), F32), vmem((HEADS, CHIP, HS), BF), vmem((HEADS, CHIP, HS), BF), vmem((HEADS, CHIP, HS), BF), vmem((CHIP, QW), BF),
        vmem((2, HS, SEQ), F32), vmem((2, 2, 4, HS, CHIP), BF), vmem((3, 2, HS, CHIP), BF), vmem((4, HS, CHIP), BF), vmem((4, HS, CHIP), BF), vmem((3, HS, CHIP), BF),
        vmem((HS, CHIP), BF), vmem((HS, CHIP), BF), vmem((2, 2, CHIP, HS), BF), vmem((2, CHIP, HS), BF),
        vmem((5, SEQ, HS), BF), vmem((SEQ, 2 * HS), BF), vmem((2 * SLICE, 2 * HS), F32),
        vmem((5, 4, 2, 2 * PART, HS), BF), vmem((5, 4, 2, 2 * PART, HS), BF), vmem((5, 3, 2, 2 * PART, HS), BF), vmem((5, 4, 2 * PART, HS), BF),
        vmem((5, 2 * PART, HS), BF), vmem((5, 2 * PART, HS), BF), vmem((5, 4, 2 * PART, HS), BF), vmem((5, 3, 2 * PART, HS), BF), vmem((5, 2, 2 * PART, HS), F32),
        vmem((2, 2, 5, 64, HS), BF),
        vmem((CHIP, D), BF), vmem((BLOCK, D), BF),
        dma((7,)), dma((6,)), dma((6,)), dma((8, 2)), dma((8, 2)), dma((2, 4, 2)), dma((2, 4, 2)), dma((2, 4)), dma((2, 4)),
        dma((2, 2, 4)), dma((2, 2, 4)), dma((HEADS,)), dma((HEADS,)), dma((HEADS,)), dma((HEADS,)),
        dma((HEADS + 1,)), dma((HEADS + 1,)), dma((2, 9, 4)), dma((5, 8)), dma((8,)), dma((8,)), dma((5, 4)), dma((5, 4)), dma((5, 4)), dma((5, 4)),
        dma((2, 2)), dma((2, 2)),
    ]
    in_vmem, anywhere = pl.BlockSpec(memory_space=pltpu.VMEM), pl.BlockSpec(memory_space=pl.ANY)
    raw = pl.pallas_call(
        layer,
        out_shape=(
            jax.ShapeDtypeStruct((BLOCK, QW), BF),
            jax.ShapeDtypeStruct((BLOCK, D), BF),
            jax.ShapeDtypeStruct((2, 2, 5, 64, HS), BF),
        ),
        in_specs=[anywhere] * 2 + [in_vmem] * 2 + [anywhere] * 2,
        out_specs=(in_vmem,) * 3,
        scratch_shapes=scratch,
        compiler_params=pltpu.CompilerParams(
            collective_id=0, has_side_effects=True, vmem_limit_bytes=63 * 2**20
        ),
        name="layer",
    )(hidden_in[0], out_grad[0], modality, segment, w_query[0], w_keyval[0])
    attended, grad_hidden, grad_wq, grad_wkv = pl.pallas_call(
        results,
        out_shape=(
            jax.ShapeDtypeStruct((BLOCK, QW), BF),
            jax.ShapeDtypeStruct((BLOCK, D), BF),
            jax.ShapeDtypeStruct((PART, QW), BF),
            jax.ShapeDtypeStruct((PART, 2 * KW), BF),
        ),
        in_specs=[in_vmem] * 3,
        out_specs=(in_vmem,) * 4,
        name="results",
    )(*raw)
    return attended[None], grad_hidden[None], grad_wq[None], grad_wkv[None]


def solution(mesh):
    return jax.shard_map(
        on_device,
        mesh=mesh,
        in_specs=(
            P("dp", ("ctx", "mod"), None),
            P("dp", ("ctx", "mod"), None),
            P("dp", ("ctx", "mod")),
            P("dp", None),
            P("mod", None, None),
            P("mod", None, None),
        ),
        out_specs=(
            P("dp", ("ctx", "mod"), None),
            P("dp", ("ctx", "mod"), None),
            P("mod", ("dp", "ctx"), None),
            P("mod", ("dp", "ctx"), None),
        ),
        check_vma=False,
    )
```

time: 120 us -> 95.6 us (0.80); the launches traced: 119 us -> 95.4 us
  Pallas kernels: 108 us -> 94.8 us
  local copies, waits for them, and re-layouts: 8.27 us -> 0 us
  other arithmetic: 1.36 us -> 0 us
    pallas_call x1, Pallas kernels: 108 us -> 92.2 us  [on_device(): pl.pallas_call(layer, out_shape=(jax.ShapeDtypeStruct((BLOCK, QW), BF), j...]
    unnamed x4 -> x0, local copies, waits for them, and re-layouts: 7.04 us -> none
    pallas_call x0 -> x1, Pallas kernels: none -> 2.59 us  [on_device(): pl.pallas_call(results, out_shape=(jax.ShapeDtypeStruct((BLOCK, QW), BF),...]
    broadcast_in_dim x2 -> x0, local copies, waits for them, and re-layouts: 1.23 us -> none  [the longest x1 0.63 us: on_device(): segs = jnp.broadcast_to(segment.astype(F32), (8, SEQ))]
where the time goes in v2:
time: 95.6 us; the launch traced here: 95.4 us
  Pallas kernels  94.8 us (99%)
    pallas_call x1, Pallas kernels, on_device(): pl.pallas_call(layer, out_shape=(jax.ShapeDtypeStruct((BLOCK, QW), BF), j...  92.2 us
    pallas_call x1, Pallas kernels, on_device(): pl.pallas_call(results, out_shape=(jax.ShapeDtypeStruct((BLOCK, QW), BF),...  2.59 us

profile of v2, /device:TPU:1, one launch (start us, length us, event | category | flops | bytes accessed | tf_op | source)
XLA Modules:
  0.0 95.4 jit_solution(8601021741556007620)
XLA Ops:
  0.6 92.2 %layer.1 = (bf16[128,1792]{1,0:T(8,128)(2,1)}, bf16[128,3584]{1,0:T(8,128)(2,1)}, bf16[2,2,5,64,128]{4,3,2,1,0:T(8,128)(2,1)}) custom-call(bf16[128,3584]{1,0:T(8,128)(2,1)} %bitcast.10, bf16[128,1792]{1,0:T(8,128)(2,1)} %bitcast.11, s32[1,128]{1,0:T(1,128)} %kinds.1, s32[1,2048]{1,0:T(1,128)} %segs.1, bf16[3584,1792]{1,0:T(8,128)(2,1)} %bitcast.8, ...), custom_call_target="tpu_custom_call" | custom-call | tf_op jit(solution)/shard_map/layer/pallas_call | solution.py:627
  92.8 2.6 %results.1 = (bf16[128,1792]{1,0:T(8,128)(2,1)}, bf16[128,3584]{1,0:T(8,128)(2,1)}, bf16[56,1792]{1,0:T(8,128)(2,1)}, bf16[56,512]{1,0:T(8,128)(2,1)}) custom-call(bf16[128,1792]{1,0:T(8,128)(2,1)} %get-tuple-element.11.att, bf16[128,3584]{1,0:T(8,128)(2,1)} %get-tuple-element.12.gh, bf16[2,2,5,64,128]{4,3,2,1,0:T(8,128)(2,1)} %get-tuple-element.13.fin), custom_call_target="tpu_custom_call" | custom-call | tf_op jit(solution)/shard_map/results/pallas_call | solution.py:642

commit v3 on v2

--- a/solution.py
+++ b/solution.py
@@ -19,7 +19,6 @@
 CHIP = 2 * BLOCK
 SLICE = 448
 PART = 56
-LAG = 2
 MESH = pl.DeviceIdType.MESH
 BF = jnp.bfloat16
 F32 = jnp.float32
@@ -45,10 +44,10 @@
 
 
 def layer(
-    hid_h, og_h, kinds, segs, wq, wkv,
-    attf, gh_o, finr,
-    hid, og, wq_v, wkv_v, hidf, hid_t, ogf, mods, at, kvs, kvr, kvall, qs, qr, qf, bias,
-    modv, attb, dqb, dqx, gq, acc, dkvb, dkr, dvr, dvz, dvzr, dkx, dkxr, gkv, gkvx, bg, be, cf, cs, cs1, crz, crx, cx, cxr, cz, czr, keep, fin, sb, sr,
+    hid_h, og_h, kinds_h, segs_h, wq, wkv,
+    att_o, gh_o, finr,
+    hid, og, kinds, segs, attf, ghf, wq_v, wkv_v, hidf, hid_t, ogf, mods, at, kvs, kvr, kvall, qs, qr, qf, bias,
+    modv, attb, dqb, dqx, gq, acc, dkvb, dkr, dvr, dvz, dvzr, dkx, dkxr, gkv, bg, be, cf, cs, cs1, crz, crz1, crx, cx, cxr, cz, czr, keep, fin, sb, sr,
     w_sem, pair_s, pair_r, mod_s, mod_r, a_s, a_r, af_s, af_r, kv_s, kv_r,
     att_s, att_r, gq_s, gq_r, bx_s, bx_r, b_s, b_r, dk_s, dk_r, c_s, c_r, cx_s, cx_r, fin_s, fin_r,
 ):
@@ -64,7 +63,8 @@
         for first, width in ((0, 512), (512, 384)):
             q_cols.append((group, first, width))
     own_loads = [
-        pltpu.make_async_copy(hid_h, hid, w_sem.at[5]), pltpu.make_async_copy(og_h, og, w_sem.at[6])
+        pltpu.make_async_copy(hid_h, hid, w_sem.at[5]), pltpu.make_async_copy(og_h, og, w_sem.at[6]),
+        pltpu.make_async_copy(kinds_h, kinds, w_sem.at[9]), pltpu.make_async_copy(segs_h, segs, w_sem.at[10]),
     ]
     loads = [pltpu.make_async_copy(wkv, wkv_v, w_sem.at[0])]
     for i, (group, first, width) in enumerate(q_cols):
@@ -107,16 +107,17 @@
     here_lanes = pl.ds(aligned(here, BLOCK), BLOCK)
     for i in range(7):
         hid_t[i * 512:(i + 1) * 512, :] = hid[:, i * 512:(i + 1) * 512].T
+    def hidden_copy(side, k, s):
+        to = (y + k) % 4
+        rows = pl.ds(pl.multiple_of((s * 4 + to) * SLICE, 64), SLICE)
+        return send(
+            hid_t.at[rows], at.at[pl.ds(s * SLICE, SLICE), here_lanes], a_s.at[side, k, s], a_r.at[side, k, s],
+            dp=(xlo if side == 0 else 1 - xlo) * 4 + to,
+        )
+
     def send_hidden(side, k):
-        to = (y + k) % 4
         for s in range(2):
-            rows = pl.ds(pl.multiple_of((s * 4 + to) * SLICE, 64), SLICE)
-            copy = send(
-                hid_t.at[rows], at.at[pl.ds(s * SLICE, SLICE), here_lanes], a_s.at[side, k, s], a_r.at[side, k, s],
-                dp=(xlo if side == 0 else 1 - xlo) * 4 + to,
-            )
-            copy.start()
-            sent.append(copy)
+            hidden_copy(side, k, s).start()
 
     for side, k in ((1, 0), (0, 1), (0, 3), (0, 2)):
         send_hidden(side, k)
@@ -137,12 +138,17 @@
                 arrived(at.at[pl.ds(s * SLICE, SLICE), lanes_of(side, k)], a_r.at[side, k, s])
         pass_hidden(side, k).start()
 
+    loads[0].wait()
+
+    def key_rows(rows):
+        made = dot(hidf[rows, :], wkv_v[...]).astype(BF)
+        for i in range(2):
+            for g in range(2):
+                kvs[i, g, rows, :] = made[:, (i * 2 + g) * HS:(i * 2 + g + 1) * HS]
+
+    key_rows(own_rows)
     hid_copy.wait_recv()
-    loads[0].wait()
-    made = dot(hidf[...], wkv_v[...]).astype(BF)
-    for i in range(2):
-        for g in range(2):
-            kvs[i, g] = made[:, (i * 2 + g) * HS:(i * 2 + g + 1) * HS]
+    key_rows(other_rows)
     copy = send(kvs.at[:, other], kvr, pair_s.at[2], pair_r.at[2], mod=other)
     copy.start()
     sent.append(copy)
@@ -216,14 +222,17 @@
             keys_from(i, 0, k)
             keys_from(i, 1, k)
 
-    def one_head(i, carry):
-        slot, target = i // 2, i % 2
-        head = target * 4 + slot
+    last = 5 - core
+
+    def head_scores(head):
+        q = qf[:, pl.ds(aligned(head, HS), HS)]
+        return dot(q, kvall[0], ((1,), (1,))) * (scale * math.log2(math.e)) + bias[...]
+
+    def rest_of_head(head, scores):
         lanes = pl.ds(aligned(head, HS), HS)
         full_lanes = pl.ds(aligned(core * HEADS + head, HS), HS)
         q, go = qf[:, lanes], ogf[:, lanes]
         keys, values = kvall[0], kvall[1]
-        scores = dot(q, keys, ((1,), (1,))) * (scale * math.log2(math.e)) + bias[...]
         top = jnp.max(scores, axis=1, keepdims=True)
         weights = jnp.exp2(scores - top)
         total = jnp.sum(weights, axis=1, keepdims=True)
@@ -245,16 +254,27 @@
         gq[:, full_lanes] = dq
         copy = send(dqb.at[head], gq.at[:, full_lanes], gq_s.at[head], gq_r.at[head], mod=other)
         copy.start()
-        spread_grads(i, head, target, slot)
         acc[0] += dot(q.T, dscore)
         acc[1] += dot((go32 * inv).astype(BF).T, low)
 
-        @pl.when(i == 2)
-        def _():
-            for k in (0, 1, 3, 2):
+    def two_heads(p, carry):
+        first, second = head_scores(p), head_scores(4 + p)
+        rest_of_head(p, first)
+        rest_of_head(4 + p, second)
+        spread_grads(p, 0, p)
+        spread_grads(4 + p, 1, p)
+
+        @pl.when(jnp.logical_and(home, p == 2))
+        def _():
+            relay_grads(0)
+            relay_grads(1)
+
+        @pl.when(p == 1)
+        def _():
+            for k in range(4):
                 relay_hidden(0, k)
 
-        @pl.when(i == 4)
+        @pl.when(p == 2)
         def _():
             for k in (0, 2, 1, 3):
                 relay_hidden(1, k)
@@ -266,8 +286,33 @@
     def cross(head):
         return send(dqb.at[head], dqx.at[head], bx_s.at[head], bx_r.at[head], dp=(1 - xlo) * 4 + y)
 
-    def cross_kv():
-        return send(gkv.at[:, core], gkvx, bx_s.at[HEADS], bx_r.at[HEADS], dp=(1 - xlo) * 4 + y)
+    def straight(src, target, slot, sems, k):
+        rows = pl.ds(aligned(dp, CHIP), CHIP)
+        return send(
+            src, bg.at[slot, rows], sems.at[k], b_r.at[slot, dp], dp=core * 4 + (y + k) % 4, mod=target
+        )
+
+    def straight_out(src, target, slot, sems):
+        at_home = jnp.logical_and(home, target == core)
+        rows = pl.ds(aligned(dp, CHIP), CHIP)
+        for k in (1, 3, 2):
+            straight(src, target, slot, sems, k).start()
+
+        @pl.when(at_home)
+        def _():
+            pltpu.make_async_copy(src, bg.at[slot, rows], b_r.at[slot, dp]).start()
+
+        @pl.when(jnp.logical_not(at_home))
+        def _():
+            straight(src, target, slot, sems, 0).start()
+
+    def straight_sent(src, target, slot, sems):
+        for k in (1, 3, 2):
+            straight(src, target, slot, sems, k).wait_send()
+
+        @pl.when(jnp.logical_not(jnp.logical_and(home, target == core)))
+        def _():
+            straight(src, target, slot, sems, 0).wait_send()
 
     def fan(src, side, target, slot, sems, k):
         rows = pl.ds(pl.multiple_of((side * 4 + y) * CHIP, CHIP), CHIP)
@@ -302,7 +347,7 @@
         arrived(dqx.at[head], bx_r.at[head])
         fan_out(dqx.at[head], 1 - xlo, target, slot, b_s.at[1, head])
 
-    def spread_grads(i, head, target, slot):
+    def spread_grads(head, target, slot):
         @pl.when(jnp.logical_not(home))
         def _():
             cross(head).start()
@@ -310,10 +355,6 @@
         @pl.when(home)
         def _():
             fan_out(dqb.at[head], xlo, target, slot, b_s.at[0, head])
-
-            @pl.when(i >= LAG)
-            def _():
-                relay_grads(i - LAG)
 
     def block_sums(slot):
         for source in range(8):
@@ -338,57 +379,83 @@
         to = (z + k) % 4
         return send(cs.at[slot, to], crz.at[slot, k - 1], c_s.at[slot, k], c_r.at[slot, k], ctx=xhi * 4 + to)
 
-    def x_leg(slot):
-        return send(cs1.at[slot, :, 1 - xhi], crx.at[slot], c_s.at[slot, 0], c_r.at[slot, 0], ctx=xctx)
+    def z_leg1(slot, k):
+        to = (z + k) % 4
+        return send(cs1.at[slot, to], crz1.at[slot, k - 1], c_s.at[slot, 3 + k], c_r.at[slot, 3 + k], ctx=xhi * 4 + to)
+
+    def x_leg():
+        return send(cs1.at[last - 1, :, 1 - xhi], crx, c_s.at[last - 1, 0], c_r.at[last - 1, 0], ctx=xctx)
 
     def then_x(slot):
-        return send(cx.at[slot], cxr.at[slot], cx_s.at[slot, 0], cx_r.at[slot, 0], ctx=xctx)
-
-    def then_z(slot, k):
+        return send(cx.at[slot, 0], cxr.at[slot, 0], cx_s.at[slot, 0], cx_r.at[slot, 0], ctx=xctx)
+
+    def then_x1(slot):
+        return send(cx.at[slot, 1], cxr.at[slot, 1], cx_s.at[slot, 1], cx_r.at[slot, 1], ctx=xctx)
+
+    def then_z(k):
         to = (z + k) % 4
-        return send(cz.at[slot, to], czr.at[slot, k - 1], cx_s.at[slot, k], cx_r.at[slot, k], ctx=xhi * 4 + to)
-
-    def z_legs(slot):
+        return send(cz.at[to], czr.at[k - 1], cx_s.at[5, k], cx_r.at[5, k], ctx=xhi * 4 + to)
+
+    def first_leg(slot):
         for k in (1, 3, 2):
             z_leg(slot, k).start()
-
-    def x_legs(slot):
-        x_leg(slot).start()
-
-    def first_leg(slot):
-        x_legs(slot)
-        z_legs(slot)
+            z_leg1(slot, k).start()
+
+    def last_first_leg():
+        x_leg().start()
+        for k in (1, 3, 2):
+            z_leg(last - 1, k).start()
+
+    def over_z_sums(mine, came, slot, half):
+        total = mine[slot, z, half].astype(F32)
+        for k in range(3):
+            total += came[slot, k, half].astype(F32)
+        return total
 
     def second_leg(slot):
-        arrived(crx.at[slot], c_r.at[slot, 0])
+        for k in (1, 3, 2):
+            arrived(crz.at[slot, k - 1], c_r.at[slot, k])
+            arrived(crz1.at[slot, k - 1], c_r.at[slot, 3 + k])
+        cx[slot, 0] = over_z_sums(cs, crz, slot, 1 - xhi).astype(BF)
+        then_x(slot).start()
+        cx[slot, 1] = over_z_sums(cs1, crz1, slot, 1 - xhi).astype(BF)
+        then_x1(slot).start()
+        keep[slot, 0] = over_z_sums(cs, crz, slot, xhi)
+        keep[slot, 1] = over_z_sums(cs1, crz1, slot, xhi)
+
+    def last_second_leg():
+        slot = last - 1
+        for k in (1, 3, 2):
+            arrived(crz.at[slot, k - 1], c_r.at[slot, k])
+        cx[slot, 0] = over_z_sums(cs, crz, slot, 1 - xhi).astype(BF)
+        then_x(slot).start()
+        arrived(crx, c_r.at[slot, 0])
         for k in (1, 3, 2):
             to = (z + k) % 4
-            cz[slot, to] = (cs1[slot, to, xhi].astype(F32) + crx[slot, to].astype(F32)).astype(BF)
-            then_z(slot, k).start()
-        keep[slot, 1] = cs1[slot, z, xhi].astype(F32) + crx[slot, z].astype(F32)
-        for k in (1, 3, 2):
-            arrived(crz.at[slot, k - 1], c_r.at[slot, k])
-        total = cs[slot, z, 1 - xhi].astype(F32)
-        for k in range(3):
-            total += crz[slot, k, 1 - xhi].astype(F32)
-        cx[slot] = total.astype(BF)
-        then_x(slot).start()
-        total = cs[slot, z, xhi].astype(F32)
-        for k in range(3):
-            total += crz[slot, k, xhi].astype(F32)
-        keep[slot, 0] = total
-
-    def last_leg(slot):
-        for k in (1, 3, 2):
-            arrived(czr.at[slot, k - 1], cx_r.at[slot, k])
-        arrived(cxr.at[slot], cx_r.at[slot, 0])
-        second = keep[slot, 1]
-        for k in range(3):
-            second += czr[slot, k].astype(F32)
-        for e, total in enumerate((keep[slot, 0] + cxr[slot].astype(F32), second)):
+            cz[to] = (cs1[slot, to, xhi].astype(F32) + crx[to].astype(F32)).astype(BF)
+            then_z(k).start()
+        keep[slot, 0] = over_z_sums(cs, crz, slot, xhi)
+        keep[slot, 1] = cs1[slot, z, xhi].astype(F32) + crx[z].astype(F32)
+
+    def finish(slot, totals):
+        for e, total in enumerate(totals):
             for s in range(2):
                 padded = jnp.concatenate([total[s * PART:(s + 1) * PART], jnp.zeros((8, HS), F32)], axis=0)
-                fin[s, e, slot] = padded.astype(BF)
+                fin[slot, s, e] = padded.astype(BF)
+
+    def last_leg(slot):
+        arrived(cxr.at[slot, 0], cx_r.at[slot, 0])
+        arrived(cxr.at[slot, 1], cx_r.at[slot, 1])
+        finish(slot, [keep[slot, e] + cxr[slot, e].astype(F32) for e in range(2)])
+
+    def last_last_leg():
+        slot = last - 1
+        arrived(cxr.at[slot, 0], cx_r.at[slot, 0])
+        second = keep[slot, 1]
+        for k in (1, 3, 2):
+            arrived(czr.at[k - 1], cx_r.at[5, k])
+            second += czr[k - 1].astype(F32)
+        finish(slot, [keep[slot, 0] + cxr[slot, 0].astype(F32), second])
 
     def each(step):
         def run(slot, carry):
@@ -397,12 +464,9 @@
 
         return run
 
-    lax.fori_loop(0, HEADS, one_head, 0)
-
-    @pl.when(home)
-    def _():
-        for i in range(HEADS - LAG, HEADS):
-            relay_grads(i)
+    lax.fori_loop(0, 3, two_heads, 0)
+    rest_of_head(3, head_scores(3))
+    spread_grads(3, 0, 3)
 
     for c in range(8):
         for i in range(2):
@@ -415,7 +479,12 @@
         copy.start()
         sent.append(copy)
 
-    last = 5 - core
+
+    @pl.when(home)
+    def _():
+        for i in (2, 3):
+            relay_grads(i)
+
     for side in range(2):
         for k in range(4):
             lanes = pl.ds(
@@ -424,7 +493,16 @@
             )
             arrived(at.at[:, lanes], af_r.at[side, k])
     other_kinds()
-    lax.fori_loop(0, 2, each(block_sums), 0)
+
+    def block_and_legs(slot):
+        block_sums(slot)
+        first_leg(slot)
+
+    lax.fori_loop(core // 2, 1, each(block_and_legs), 0)
+    for head in range(HEADS):
+        arrived(attf.at[:, pl.ds(aligned(other * HEADS + head, HS), HS)], att_r.at[head])
+    att_out = pltpu.make_async_copy(attf, att_o, w_sem.at[7])
+    att_out.start()
     for head in range(HEADS):
         arrived(gq.at[:, pl.ds(aligned(other * HEADS + head, HS), HS)], gq_r.at[head])
 
@@ -459,8 +537,12 @@
     dk_copy = send(dkx, dkxr, dk_s.at[4], dk_r.at[4], ctx=xctx)
     dk_copy.start()
     sent.append(dk_copy)
-    lax.fori_loop(0, 2, each(first_leg), 0)
-    lax.fori_loop(2, last - 1, each(block_sums), 0)
+    @pl.when(home)
+    def _():
+        for i in (4, 5, 6):
+            relay_grads(i)
+
+    lax.fori_loop(1 + core // 2, 2, each(block_and_legs), 0)
     dk = over_z(xhi)
     dv = acc[1, :, pl.ds(pl.multiple_of((xhi * 4 + z) * CHIP, CHIP), CHIP)] + dvr[z].astype(F32)
     for k in (1, 3, 2):
@@ -474,24 +556,10 @@
     gkv_copy = send(gkv.at[:, core], gkv.at[:, core], pair_s.at[4], pair_r.at[4], mod=other)
     gkv_copy.start()
     sent.append(gkv_copy)
-
-    @pl.when(jnp.logical_not(home))
-    def _():
-        cross_kv().start()
-
-    @pl.when(home)
-    def _():
-        for i, target, slot in ((0, 0, 4), (1, 1, 3)):
-            fan_out(gkv.at[i, core], xlo, target, slot, b_s.at[0, HEADS + i])
-
-    lax.fori_loop(2, last - 1, each(first_leg), 0)
-    lax.fori_loop(0, 2, each(second_leg), 0)
-
-    @pl.when(home)
-    def _():
-        arrived(gkvx, bx_r.at[HEADS])
-        for i, target, slot in ((0, 0, 4), (1, 1, 3)):
-            fan_out(gkvx.at[i], 1 - xlo, target, slot, b_s.at[1, HEADS + i])
+    for i, target, slot in ((0, 0, 4), (1, 1, 3)):
+        straight_out(gkv.at[i, core], target, slot, b_s.at[0, HEADS + i])
+
+    lax.fori_loop(2, last - 1, each(block_and_legs), 0)
 
     arrived(gkv.at[:, other], pair_r.at[4])
     grads_kv = jnp.concatenate([gkv[0, 0], gkv[0, 1], gkv[1, 0], gkv[1, 1]], axis=1)
@@ -502,38 +570,52 @@
     home_copy = send(sb.at[other_rows], sr, pair_s.at[5], pair_r.at[5], mod=other)
     home_copy.start()
     sent.append(home_copy)
-
-    block_sums(last - 1)
-    first_leg(last - 1)
-
-    fin[...] = jnp.zeros_like(fin)
-    lax.fori_loop(2, last, each(second_leg), 0)
-    lax.fori_loop(0, last, each(last_leg), 0)
-    for s in range(2):
-        for e in range(2):
-            at_home = jnp.logical_and(xlo == s, core == e)
-            copy = send(
-                fin.at[s, e], finr.at[xlo, core], fin_s.at[s, e], fin_r.at[xlo, core], dp=s * 4 + y, mod=e
-            )
-
-            @pl.when(at_home)
-            def _():
-                pltpu.make_async_copy(fin.at[s, e], finr.at[xlo, core], fin_r.at[xlo, core]).start()
-
-            @pl.when(jnp.logical_not(at_home))
-            def _():
-                copy.start()
-
-    for head in range(HEADS):
-        lanes = pl.ds(aligned(other * HEADS + head, HS), HS)
-        arrived(attf.at[:, lanes], att_r.at[head])
+    lax.fori_loop(last - 1, last, each(block_sums), 0)
+    last_first_leg()
     arrived(sr, pair_r.at[5])
     pick = jnp.broadcast_to(mods[here][0:1, 0:1], (BLOCK, D)) == expert
-    gh_o[...] = jnp.where(pick, sb[own_rows, :], sr[...])
-
+    ghf[...] = jnp.where(pick, sb[own_rows, :], sr[...])
+    gh_out = pltpu.make_async_copy(ghf, gh_o, w_sem.at[8])
+    gh_out.start()
+    lax.fori_loop(0, 2, each(second_leg), 0)
+
+    def results_out(slot):
+        for s in range(2):
+            for e in range(2):
+                at_home = jnp.logical_and(xlo == s, core == e)
+
+                @pl.when(at_home)
+                def _():
+                    pltpu.make_async_copy(
+                        fin.at[slot, s, e], finr.at[xlo, core, slot], fin_r.at[xlo, core, slot]
+                    ).start()
+
+                @pl.when(jnp.logical_not(at_home))
+                def _():
+                    result_copy(slot, s, e).start()
+
+    def result_copy(slot, s, e):
+        return send(
+            fin.at[slot, s, e], finr.at[xlo, core, slot], fin_s.at[slot, s, e], fin_r.at[xlo, core, slot],
+            dp=s * 4 + y, mod=e,
+        )
+
+    def last_step(slot):
+        last_leg(slot)
+        results_out(slot)
+
+    lax.fori_loop(2, last - 1, each(second_leg), 0)
+    last_second_leg()
+    lax.fori_loop(core // 2, last - 1, each(last_step), 0)
+    last_last_leg()
+    results_out(last - 1)
+
+    att_out.wait()
+    gh_out.wait()
     for g in range(2):
         for c in range(2):
-            arrived(finr.at[g, c], fin_r.at[g, c])
+            for slot in range(5 - c):
+                arrived(finr.at[g, c, slot], fin_r.at[g, c, slot])
 
     for copy in sent:
         copy.wait_send()
@@ -560,35 +642,36 @@
     for side in range(2):
         for k in range(4):
             pass_hidden(side, k).wait_send()
-
-    @pl.when(jnp.logical_not(home))
-    def _():
-        cross_kv().wait_send()
-
-    @pl.when(home)
-    def _():
-        for i, target, slot in ((0, 0, 4), (1, 1, 3)):
-            fan_sent(gkv.at[i, core], xlo, target, slot, b_s.at[0, HEADS + i])
-            fan_sent(gkvx.at[i], 1 - xlo, target, slot, b_s.at[1, HEADS + i])
+            if side or k:
+                for s in range(2):
+                    hidden_copy(side, k, s).wait_send()
+    for i, target, slot in ((0, 0, 4), (1, 1, 3)):
+        straight_sent(gkv.at[i, core], target, slot, b_s.at[0, HEADS + i])
 
     def blocks_sent(slot, carry):
-        x_leg(slot).wait_send()
         then_x(slot).wait_send()
         for k in (1, 3, 2):
             z_leg(slot, k).wait_send()
-            then_z(slot, k).wait_send()
+
+        @pl.when(slot < last - 1)
+        def _():
+            then_x1(slot).wait_send()
+            for k in (1, 3, 2):
+                z_leg1(slot, k).wait_send()
+
+        for s in range(2):
+            for e in range(2):
+
+                @pl.when(jnp.logical_not(jnp.logical_and(xlo == s, core == e)))
+                def _():
+                    result_copy(slot, s, e).wait_send()
+
         return carry
 
     lax.fori_loop(0, last, blocks_sent, 0)
-    for s in range(2):
-        for e in range(2):
-            copy = send(
-                fin.at[s, e], finr.at[xlo, core], fin_s.at[s, e], fin_r.at[xlo, core], dp=s * 4 + y, mod=e
-            )
-
-            @pl.when(jnp.logical_not(jnp.logical_and(xlo == s, core == e)))
-            def _():
-                copy.wait_send()
+    x_leg().wait_send()
+    for k in (1, 3, 2):
+        then_z(k).wait_send()
 
 
 def results(att, gh, fin, att_o, gh_o, gwq_o, gwkv_o):
@@ -605,23 +688,24 @@
 def on_device(hidden_in, out_grad, modality, segment, w_query, w_keyval):
     vmem, dma = pltpu.VMEM, pltpu.SemaphoreType.DMA
     scratch = [
-        vmem((BLOCK, D), BF), vmem((BLOCK, QW), BF), vmem((D, QW), BF), vmem((D, 2 * KW), BF),
+        vmem((BLOCK, D), BF), vmem((BLOCK, QW), BF), vmem((1, BLOCK), jnp.int32), vmem((1, SEQ), jnp.int32),
+        vmem((BLOCK, QW), BF), vmem((BLOCK, D), BF), vmem((D, QW), BF), vmem((D, 2 * KW), BF),
         vmem((CHIP, D), BF), vmem((D, BLOCK), BF), vmem((CHIP, GW), BF), vmem((16, 8, HS), F32),
         vmem((2 * SLICE, SEQ), BF),
         vmem((2, 2, CHIP, HS), BF), vmem((2, CHIP, HS), BF), vmem((2, SEQ, HS), BF),
         vmem((2, CHIP, GW), BF), vmem((CHIP, GW), BF), vmem((CHIP, GW), BF), vmem((CHIP, SEQ), F32),
         vmem((8, BLOCK), F32), vmem((HEADS, CHIP, HS), BF), vmem((HEADS, CHIP, HS), BF), vmem((HEADS, CHIP, HS), BF), vmem((CHIP, QW), BF),
         vmem((2, HS, SEQ), F32), vmem((2, 2, 4, HS, CHIP), BF), vmem((3, 2, HS, CHIP), BF), vmem((4, HS, CHIP), BF), vmem((4, HS, CHIP), BF), vmem((3, HS, CHIP), BF),
-        vmem((HS, CHIP), BF), vmem((HS, CHIP), BF), vmem((2, 2, CHIP, HS), BF), vmem((2, CHIP, HS), BF),
+        vmem((HS, CHIP), BF), vmem((HS, CHIP), BF), vmem((2, 2, CHIP, HS), BF),
         vmem((5, SEQ, HS), BF), vmem((SEQ, 2 * HS), BF), vmem((2 * SLICE, 2 * HS), F32),
-        vmem((5, 4, 2, 2 * PART, HS), BF), vmem((5, 4, 2, 2 * PART, HS), BF), vmem((5, 3, 2, 2 * PART, HS), BF), vmem((5, 4, 2 * PART, HS), BF),
-        vmem((5, 2 * PART, HS), BF), vmem((5, 2 * PART, HS), BF), vmem((5, 4, 2 * PART, HS), BF), vmem((5, 3, 2 * PART, HS), BF), vmem((5, 2, 2 * PART, HS), F32),
-        vmem((2, 2, 5, 64, HS), BF),
+        vmem((5, 4, 2, 2 * PART, HS), BF), vmem((5, 4, 2, 2 * PART, HS), BF), vmem((5, 3, 2, 2 * PART, HS), BF), vmem((5, 3, 2, 2 * PART, HS), BF), vmem((4, 2 * PART, HS), BF),
+        vmem((5, 2, 2 * PART, HS), BF), vmem((5, 2, 2 * PART, HS), BF), vmem((4, 2 * PART, HS), BF), vmem((3, 2 * PART, HS), BF), vmem((5, 2, 2 * PART, HS), F32),
+        vmem((5, 2, 2, 64, HS), BF),
         vmem((CHIP, D), BF), vmem((BLOCK, D), BF),
-        dma((7,)), dma((6,)), dma((6,)), dma((8, 2)), dma((8, 2)), dma((2, 4, 2)), dma((2, 4, 2)), dma((2, 4)), dma((2, 4)),
+        dma((11,)), dma((6,)), dma((6,)), dma((8, 2)), dma((8, 2)), dma((2, 4, 2)), dma((2, 4, 2)), dma((2, 4)), dma((2, 4)),
         dma((2, 2, 4)), dma((2, 2, 4)), dma((HEADS,)), dma((HEADS,)), dma((HEADS,)), dma((HEADS,)),
-        dma((HEADS + 1,)), dma((HEADS + 1,)), dma((2, 9, 4)), dma((5, 8)), dma((8,)), dma((8,)), dma((5, 4)), dma((5, 4)), dma((5, 4)), dma((5, 4)),
-        dma((2, 2)), dma((2, 2)),
+        dma((HEADS,)), dma((HEADS,)), dma((2, 9, 4)), dma((5, 8)), dma((8,)), dma((8,)), dma((5, 7)), dma((5, 7)), dma((6, 4)), dma((6, 4)),
+        dma((5, 2, 2)), dma((2, 2, 5)),
     ]
     in_vmem, anywhere = pl.BlockSpec(memory_space=pltpu.VMEM), pl.BlockSpec(memory_space=pl.ANY)
     raw = pl.pallas_call(
@@ -631,8 +715,8 @@
             jax.ShapeDtypeStruct((BLOCK, D), BF),
             jax.ShapeDtypeStruct((2, 2, 5, 64, HS), BF),
         ),
-        in_specs=[anywhere] * 2 + [in_vmem] * 2 + [anywhere] * 2,
-        out_specs=(in_vmem,) * 3,
+        in_specs=[anywhere] * 6,
+        out_specs=(anywhere, anywhere, in_vmem),
         scratch_shapes=scratch,
         compiler_params=pltpu.CompilerParams(
             collective_id=0, has_side_effects=True, vmem_limit_bytes=63 * 2**20

time: 95.6 us -> 86.7 us (0.907)
  Pallas kernels: 94.8 us -> 86 us
    pallas_call x1, Pallas kernels: 92.2 us -> 83.4 us  [on_device(): pl.pallas_call(layer, out_shape=(jax.ShapeDtypeStruct((BLOCK, QW), BF), j...]
where the time goes in v3:
time: 86.7 us; the launch traced here: 86.6 us
  Pallas kernels  86 us (99%)
    pallas_call x1, Pallas kernels, on_device(): pl.pallas_call(layer, out_shape=(jax.ShapeDtypeStruct((BLOCK, QW), BF), j...  83.4 us
    pallas_call x1, Pallas kernels, on_device(): pl.pallas_call(results, out_shape=(jax.ShapeDtypeStruct((BLOCK, QW), BF),...  2.59 us

profile of v3, /device:TPU:1, one launch (start us, length us, event | category | flops | bytes accessed | tf_op | source)
XLA Modules:
  0.0 86.6 jit_solution(1370338028487176453)
XLA Ops:
  0.6 83.4 %layer.1 = (bf16[128,1792]{1,0:T(8,128)(2,1)}, bf16[128,3584]{1,0:T(8,128)(2,1)}, bf16[2,2,5,64,128]{4,3,2,1,0:T(8,128)(2,1)}) custom-call(bf16[128,3584]{1,0:T(8,128)(2,1)} %bitcast.10, bf16[128,1792]{1,0:T(8,128)(2,1)} %bitcast.11, s32[1,128]{1,0:T(1,128)} %kinds_h.1, s32[1,2048]{1,0:T(1,128)} %segs_h.1, bf16[3584,1792]{1,0:T(8,128)(2,1)} %bitcast.8, ...), custom_call_target="tpu_custom_call" | custom-call | tf_op jit(solution)/shard_map/layer/pallas_call | solution.py:711
  84.0 2.6 %results.1 = (bf16[128,1792]{1,0:T(8,128)(2,1)}, bf16[128,3584]{1,0:T(8,128)(2,1)}, bf16[56,1792]{1,0:T(8,128)(2,1)}, bf16[56,512]{1,0:T(8,128)(2,1)}) custom-call(bf16[128,1792]{1,0:T(8,128)(2,1)} %get-tuple-element.11.att, bf16[128,3584]{1,0:T(8,128)(2,1)} %get-tuple-element.12.gh, bf16[2,2,5,64,128]{4,3,2,1,0:T(8,128)(2,1)} %get-tuple-element.13.fin), custom_call_target="tpu_custom_call" | custom-call | tf_op jit(solution)/shard_map/results/pallas_call | solution.py:726

commit v4 on v3

--- a/solution.py
+++ b/solution.py
@@ -47,7 +47,7 @@
     hid_h, og_h, kinds_h, segs_h, wq, wkv,
     att_o, gh_o, finr,
     hid, og, kinds, segs, attf, ghf, wq_v, wkv_v, hidf, hid_t, ogf, mods, at, kvs, kvr, kvall, qs, qr, qf, bias,
-    modv, attb, dqb, dqx, gq, acc, dkvb, dkr, dvr, dvz, dvzr, dkx, dkxr, gkv, bg, be, cf, cs, cs1, crz, crz1, crx, cx, cxr, cz, czr, keep, fin, sb, sr,
+    modv, attb, dqb, dqx, gq, acc, dkvb, dkr, dvr, dvz, dvzr, dkx, dkxr, gkv, bg, be, cf, cs, cs1, crz, crx, cx, cxr, cz, czr, keep, fin, sb, sr,
     w_sem, pair_s, pair_r, mod_s, mod_r, a_s, a_r, af_s, af_r, kv_s, kv_r,
     att_s, att_r, gq_s, gq_r, bx_s, bx_r, b_s, b_r, dk_s, dk_r, c_s, c_r, cx_s, cx_r, fin_s, fin_r,
 ):
@@ -98,9 +98,8 @@
             if k == 0 and c == 0:
                 continue
             dev = {"dp": (dp + k) % 8, "mod": other if c else core}
-            copy = send(modv, mods.at[here], mod_s.at[k, c], mod_r.at[k, c], **dev)
+            copy = send(modv, mods.at[here], mod_s, mod_r.at[1 if k else 0], **dev)
             copy.start()
-            sent.append(copy)
     hidf[own_rows, :] = hid[...]
     ogf[own_rows, :] = og[:, pl.ds(aligned(core, GW), GW)]
 
@@ -111,7 +110,7 @@
         to = (y + k) % 4
         rows = pl.ds(pl.multiple_of((s * 4 + to) * SLICE, 64), SLICE)
         return send(
-            hid_t.at[rows], at.at[pl.ds(s * SLICE, SLICE), here_lanes], a_s.at[side, k, s], a_r.at[side, k, s],
+            hid_t.at[rows], at.at[pl.ds(s * SLICE, SLICE), here_lanes], a_s, a_r.at[side, k],
             dp=(xlo if side == 0 else 1 - xlo) * 4 + to,
         )
 
@@ -130,12 +129,11 @@
 
     def pass_hidden(side, k):
         lanes = lanes_of(side, k)
-        return send(at.at[:, lanes], at.at[:, lanes], af_s.at[side, k], af_r.at[side, k], mod=other)
+        return send(at.at[:, lanes], at.at[:, lanes], af_s, af_r, mod=other)
 
     def relay_hidden(side, k):
         if side or k:
-            for s in range(2):
-                arrived(at.at[pl.ds(s * SLICE, SLICE), lanes_of(side, k)], a_r.at[side, k, s])
+            arrived(at.at[:, lanes_of(side, k)], a_r.at[side, k])
         pass_hidden(side, k).start()
 
     loads[0].wait()
@@ -153,10 +151,9 @@
     copy.start()
     sent.append(copy)
     def other_kinds():
-        for k in range(1, 8):
-            for c in range(2):
-                arrived(mods.at[(dp - k + 8) % 8 * 2 + (other if c else core)], mod_r.at[k, c])
-    arrived(mods.at[dp * 2 + other], mod_r.at[0, 1])
+        arrived(mods.at[0:14], mod_r.at[1])
+
+    arrived(mods.at[dp * 2 + other], mod_r.at[0])
     mine = [
         jnp.broadcast_to(mods[dp * 2 + b][0:1, :], (BLOCK, HS)) == expert for b in range(2)
     ]
@@ -175,12 +172,11 @@
         return pl.ds(aligned((xhi if side == 0 else 1 - xhi) * 4 + (z - k + 4) % 4, CHIP), CHIP)
 
     def send_keys(i, side, k, rows, to):
-        copy = send(kvall.at[i, rows], kvall.at[i, rows], kv_s.at[i, side, k], kv_r.at[i, side, k], ctx=to)
+        copy = send(kvall.at[i, rows], kvall.at[i, rows], kv_s, kv_r.at[i if side and not k else 2], ctx=to)
         copy.start()
-        sent.append(copy)
 
     def keys_from(i, side, k):
-        arrived(kvall.at[i, rows_from(side, k)], kv_r.at[i, side, k])
+        arrived(kvall.at[i, rows_from(side, k)], kv_r.at[i])
 
     for i in range(2):
         send_keys(i, 1, 0, ctx_rows, xctx)
@@ -217,10 +213,7 @@
         pick = jnp.broadcast_to(mods[dp * 2 + b][0:1, 0:1], (BLOCK, GW)) == expert
         qf[rows, :] = jnp.where(pick, qs[core, rows, :], qr[rows, :])
     og_copy.wait_recv()
-    for i in range(2):
-        for k in (1, 3, 2):
-            keys_from(i, 0, k)
-            keys_from(i, 1, k)
+    arrived(kvall.at[:, 0:6 * CHIP], kv_r.at[2])
 
     last = 5 - core
 
@@ -241,7 +234,7 @@
         attended = (dot(low, values) * inv).astype(BF)
         attb[head] = attended
         copy = send(
-            attb.at[head, other_rows], attf.at[:, full_lanes], att_s.at[head], att_r.at[head], mod=other
+            attb.at[head, other_rows], attf.at[:, full_lanes], att_s, att_r, mod=other
         )
         copy.start()
         attf[:, full_lanes] = attb[head, own_rows, :]
@@ -252,7 +245,7 @@
         dq = (dot(dscore, keys) * scale).astype(BF)
         dqb[head] = dq
         gq[:, full_lanes] = dq
-        copy = send(dqb.at[head], gq.at[:, full_lanes], gq_s.at[head], gq_r.at[head], mod=other)
+        copy = send(dqb.at[head], gq.at[:, full_lanes], gq_s, gq_r, mod=other)
         copy.start()
         acc[0] += dot(q.T, dscore)
         acc[1] += dot((go32 * inv).astype(BF).T, low)
@@ -284,12 +277,12 @@
     home = xlo == core
 
     def cross(head):
-        return send(dqb.at[head], dqx.at[head], bx_s.at[head], bx_r.at[head], dp=(1 - xlo) * 4 + y)
+        return send(dqb.at[head], dqx.at[head], bx_s, bx_r.at[head], dp=(1 - xlo) * 4 + y)
 
     def straight(src, target, slot, sems, k):
         rows = pl.ds(aligned(dp, CHIP), CHIP)
         return send(
-            src, bg.at[slot, rows], sems.at[k], b_r.at[slot, dp], dp=core * 4 + (y + k) % 4, mod=target
+            src, bg.at[slot, rows], sems, b_r.at[slot], dp=core * 4 + (y + k) % 4, mod=target
         )
 
     def straight_out(src, target, slot, sems):
@@ -300,24 +293,16 @@
 
         @pl.when(at_home)
         def _():
-            pltpu.make_async_copy(src, bg.at[slot, rows], b_r.at[slot, dp]).start()
+            pltpu.make_async_copy(src, bg.at[slot, rows], b_r.at[slot]).start()
 
         @pl.when(jnp.logical_not(at_home))
         def _():
             straight(src, target, slot, sems, 0).start()
-
-    def straight_sent(src, target, slot, sems):
-        for k in (1, 3, 2):
-            straight(src, target, slot, sems, k).wait_send()
-
-        @pl.when(jnp.logical_not(jnp.logical_and(home, target == core)))
-        def _():
-            straight(src, target, slot, sems, 0).wait_send()
 
     def fan(src, side, target, slot, sems, k):
         rows = pl.ds(pl.multiple_of((side * 4 + y) * CHIP, CHIP), CHIP)
         return send(
-            src, bg.at[slot, rows], sems.at[k], b_r.at[slot, side * 4 + y], dp=xlo * 4 + (y + k) % 4, mod=target
+            src, bg.at[slot, rows], sems, b_r.at[slot], dp=xlo * 4 + (y + k) % 4, mod=target
         )
 
     def fan_out(src, side, target, slot, sems):
@@ -327,25 +312,17 @@
 
         @pl.when(target == core)
         def _():
-            pltpu.make_async_copy(src, bg.at[slot, rows], b_r.at[slot, side * 4 + y]).start()
+            pltpu.make_async_copy(src, bg.at[slot, rows], b_r.at[slot]).start()
 
         @pl.when(target != core)
         def _():
             fan(src, side, target, slot, sems, 0).start()
-
-    def fan_sent(src, side, target, slot, sems):
-        for k in (1, 3, 2):
-            fan(src, side, target, slot, sems, k).wait_send()
-
-        @pl.when(target != core)
-        def _():
-            fan(src, side, target, slot, sems, 0).wait_send()
 
     def relay_grads(i):
         slot, target = i // 2, i % 2
         head = target * 4 + slot
         arrived(dqx.at[head], bx_r.at[head])
-        fan_out(dqx.at[head], 1 - xlo, target, slot, b_s.at[1, head])
+        fan_out(dqx.at[head], 1 - xlo, target, slot, b_s.at[1])
 
     def spread_grads(head, target, slot):
         @pl.when(jnp.logical_not(home))
@@ -354,11 +331,10 @@
 
         @pl.when(home)
         def _():
-            fan_out(dqb.at[head], xlo, target, slot, b_s.at[0, head])
+            fan_out(dqb.at[head], xlo, target, slot, b_s.at[0])
 
     def block_sums(slot):
-        for source in range(8):
-            arrived(bg.at[slot, pl.ds(source * CHIP, CHIP)], b_r.at[slot, source])
+        arrived(bg.at[slot], b_r.at[slot])
         for t in range(16):
             rows = slice(t * BLOCK, (t + 1) * BLOCK)
             kind = mods[t][0:1, :]
@@ -377,65 +353,40 @@
 
     def z_leg(slot, k):
         to = (z + k) % 4
-        return send(cs.at[slot, to], crz.at[slot, k - 1], c_s.at[slot, k], c_r.at[slot, k], ctx=xhi * 4 + to)
-
-    def z_leg1(slot, k):
+        return send(cs.at[slot, to], crz.at[slot, k - 1], c_s.at[slot], c_r.at[slot, 1], ctx=xhi * 4 + to)
+
+    def x_leg(slot):
+        return send(cs1.at[slot, :, 1 - xhi], crx.at[slot], c_s.at[slot], c_r.at[slot, 0], ctx=xctx)
+
+    def then_x(slot):
+        return send(cx.at[slot], cxr.at[slot], cx_s.at[slot], cx_r.at[slot, 0], ctx=xctx)
+
+    def then_z(slot, k):
         to = (z + k) % 4
-        return send(cs1.at[slot, to], crz1.at[slot, k - 1], c_s.at[slot, 3 + k], c_r.at[slot, 3 + k], ctx=xhi * 4 + to)
-
-    def x_leg():
-        return send(cs1.at[last - 1, :, 1 - xhi], crx, c_s.at[last - 1, 0], c_r.at[last - 1, 0], ctx=xctx)
-
-    def then_x(slot):
-        return send(cx.at[slot, 0], cxr.at[slot, 0], cx_s.at[slot, 0], cx_r.at[slot, 0], ctx=xctx)
-
-    def then_x1(slot):
-        return send(cx.at[slot, 1], cxr.at[slot, 1], cx_s.at[slot, 1], cx_r.at[slot, 1], ctx=xctx)
-
-    def then_z(k):
-        to = (z + k) % 4
-        return send(cz.at[to], czr.at[k - 1], cx_s.at[5, k], cx_r.at[5, k], ctx=xhi * 4 + to)
+        return send(cz.at[slot, to], czr.at[slot, k - 1], cx_s.at[slot], cx_r.at[slot, 1], ctx=xhi * 4 + to)
 
     def first_leg(slot):
+        x_leg(slot).start()
         for k in (1, 3, 2):
             z_leg(slot, k).start()
-            z_leg1(slot, k).start()
-
-    def last_first_leg():
-        x_leg().start()
-        for k in (1, 3, 2):
-            z_leg(last - 1, k).start()
-
-    def over_z_sums(mine, came, slot, half):
-        total = mine[slot, z, half].astype(F32)
-        for k in range(3):
-            total += came[slot, k, half].astype(F32)
-        return total
 
     def second_leg(slot):
-        for k in (1, 3, 2):
-            arrived(crz.at[slot, k - 1], c_r.at[slot, k])
-            arrived(crz1.at[slot, k - 1], c_r.at[slot, 3 + k])
-        cx[slot, 0] = over_z_sums(cs, crz, slot, 1 - xhi).astype(BF)
-        then_x(slot).start()
-        cx[slot, 1] = over_z_sums(cs1, crz1, slot, 1 - xhi).astype(BF)
-        then_x1(slot).start()
-        keep[slot, 0] = over_z_sums(cs, crz, slot, xhi)
-        keep[slot, 1] = over_z_sums(cs1, crz1, slot, xhi)
-
-    def last_second_leg():
-        slot = last - 1
-        for k in (1, 3, 2):
-            arrived(crz.at[slot, k - 1], c_r.at[slot, k])
-        cx[slot, 0] = over_z_sums(cs, crz, slot, 1 - xhi).astype(BF)
-        then_x(slot).start()
-        arrived(crx, c_r.at[slot, 0])
+        arrived(crx.at[slot], c_r.at[slot, 0])
         for k in (1, 3, 2):
             to = (z + k) % 4
-            cz[to] = (cs1[slot, to, xhi].astype(F32) + crx[to].astype(F32)).astype(BF)
-            then_z(k).start()
-        keep[slot, 0] = over_z_sums(cs, crz, slot, xhi)
-        keep[slot, 1] = cs1[slot, z, xhi].astype(F32) + crx[z].astype(F32)
+            cz[slot, to] = (cs1[slot, to, xhi].astype(F32) + crx[slot, to].astype(F32)).astype(BF)
+            then_z(slot, k).start()
+        keep[slot, 1] = cs1[slot, z, xhi].astype(F32) + crx[slot, z].astype(F32)
+        arrived(crz.at[slot], c_r.at[slot, 1])
+        total = cs[slot, z, 1 - xhi].astype(F32)
+        for k in range(3):
+            total += crz[slot, k, 1 - xhi].astype(F32)
+        cx[slot] = total.astype(BF)
+        then_x(slot).start()
+        total = cs[slot, z, xhi].astype(F32)
+        for k in range(3):
+            total += crz[slot, k, xhi].astype(F32)
+        keep[slot, 0] = total
 
     def finish(slot, totals):
         for e, total in enumerate(totals):
@@ -444,18 +395,12 @@
                 fin[slot, s, e] = padded.astype(BF)
 
     def last_leg(slot):
-        arrived(cxr.at[slot, 0], cx_r.at[slot, 0])
-        arrived(cxr.at[slot, 1], cx_r.at[slot, 1])
-        finish(slot, [keep[slot, e] + cxr[slot, e].astype(F32) for e in range(2)])
-
-    def last_last_leg():
-        slot = last - 1
-        arrived(cxr.at[slot, 0], cx_r.at[slot, 0])
+        arrived(cxr.at[slot], cx_r.at[slot, 0])
         second = keep[slot, 1]
-        for k in (1, 3, 2):
-            arrived(czr.at[k - 1], cx_r.at[5, k])
-            second += czr[k - 1].astype(F32)
-        finish(slot, [keep[slot, 0] + cxr[slot, 0].astype(F32), second])
+        arrived(czr.at[slot], cx_r.at[slot, 1])
+        for k in range(3):
+            second += czr[slot, k].astype(F32)
+        finish(slot, [keep[slot, 0] + cxr[slot].astype(F32), second])
 
     def each(step):
         def run(slot, carry):
@@ -474,10 +419,9 @@
     copies = [send(dkvb.at[1, 1 - xhi], dvr, dk_s.at[0], dk_r.at[0], ctx=xctx)]
     for k in (1, 3, 2):
         to = (z + k) % 4
-        copies.append(send(dkvb.at[0, :, to], dkr.at[k - 1], dk_s.at[k], dk_r.at[k], ctx=xhi * 4 + to))
+        copies.append(send(dkvb.at[0, :, to], dkr.at[k - 1], dk_s.at[1], dk_r.at[1], ctx=xhi * 4 + to))
     for copy in copies:
         copy.start()
-        sent.append(copy)
 
 
     @pl.when(home)
@@ -485,26 +429,10 @@
         for i in (2, 3):
             relay_grads(i)
 
-    for side in range(2):
-        for k in range(4):
-            lanes = pl.ds(
-                pl.multiple_of((((xlo if side == 0 else 1 - xlo) * 4 + (y - k + 4) % 4) * 2 + other) * BLOCK, BLOCK),
-                BLOCK,
-            )
-            arrived(at.at[:, lanes], af_r.at[side, k])
-    other_kinds()
-
-    def block_and_legs(slot):
-        block_sums(slot)
-        first_leg(slot)
-
-    lax.fori_loop(core // 2, 1, each(block_and_legs), 0)
-    for head in range(HEADS):
-        arrived(attf.at[:, pl.ds(aligned(other * HEADS + head, HS), HS)], att_r.at[head])
+    arrived(attf.at[:, pl.ds(aligned(other, GW), GW)], att_r)
     att_out = pltpu.make_async_copy(attf, att_o, w_sem.at[7])
     att_out.start()
-    for head in range(HEADS):
-        arrived(gq.at[:, pl.ds(aligned(other * HEADS + head, HS), HS)], gq_r.at[head])
+    arrived(gq.at[:, pl.ds(aligned(other, GW), GW)], gq_r)
 
     def spread(i, carry):
         rows = pl.ds(aligned(i, 512), 512)
@@ -515,17 +443,23 @@
         return carry
 
     lax.fori_loop(0, 7, spread, 0)
+    arrived(at.at[:, 0:8 * BLOCK], af_r)
+    other_kinds()
+
+    def block_and_legs(slot):
+        block_sums(slot)
+        first_leg(slot)
+
+    lax.fori_loop(core // 2, 1, each(block_sums), 0)
 
     copies[0].wait_recv()
     for k in (1, 3, 2):
         to = (z + k) % 4
         lanes = pl.ds(pl.multiple_of((xhi * 4 + to) * CHIP, CHIP), CHIP)
         dvz[to] = (acc[1, :, lanes] + dvr[to].astype(F32)).astype(BF)
-        copy = send(dvz.at[to], dvzr.at[k - 1], dk_s.at[4 + k], dk_r.at[4 + k], ctx=xhi * 4 + to)
+        copy = send(dvz.at[to], dvzr.at[k - 1], dk_s.at[0], dk_r.at[2], ctx=xhi * 4 + to)
         copy.start()
-        sent.append(copy)
-    for k in (1, 3, 2):
-        arrived(dkr.at[k - 1], dk_r.at[k])
+    arrived(dkr, dk_r.at[1])
 
     def over_z(half):
         total = acc[0, :, pl.ds(pl.multiple_of((half * 4 + z) * CHIP, CHIP), CHIP)]
@@ -534,19 +468,18 @@
         return total
 
     dkx[...] = over_z(1 - xhi).astype(BF)
-    dk_copy = send(dkx, dkxr, dk_s.at[4], dk_r.at[4], ctx=xctx)
+    dk_copy = send(dkx, dkxr, dk_s.at[0], dk_r.at[3], ctx=xctx)
     dk_copy.start()
-    sent.append(dk_copy)
+    first_leg(0)
+    lax.fori_loop(1 + core // 2, 2, each(block_and_legs), 0)
     @pl.when(home)
     def _():
         for i in (4, 5, 6):
             relay_grads(i)
 
-    lax.fori_loop(1 + core // 2, 2, each(block_and_legs), 0)
     dk = over_z(xhi)
     dv = acc[1, :, pl.ds(pl.multiple_of((xhi * 4 + z) * CHIP, CHIP), CHIP)] + dvr[z].astype(F32)
-    for k in (1, 3, 2):
-        arrived(dvzr.at[k - 1], dk_r.at[4 + k])
+    arrived(dvzr, dk_r.at[2])
     for k in range(3):
         dv += dvzr[k].astype(F32)
     gkv[1, core] = dv.T.astype(BF)
@@ -557,7 +490,7 @@
     gkv_copy.start()
     sent.append(gkv_copy)
     for i, target, slot in ((0, 0, 4), (1, 1, 3)):
-        straight_out(gkv.at[i, core], target, slot, b_s.at[0, HEADS + i])
+        straight_out(gkv.at[i, core], target, slot, b_s.at[2])
 
     lax.fori_loop(2, last - 1, each(block_and_legs), 0)
 
@@ -570,8 +503,7 @@
     home_copy = send(sb.at[other_rows], sr, pair_s.at[5], pair_r.at[5], mod=other)
     home_copy.start()
     sent.append(home_copy)
-    lax.fori_loop(last - 1, last, each(block_sums), 0)
-    last_first_leg()
+    lax.fori_loop(last - 1, last, each(block_and_legs), 0)
     arrived(sr, pair_r.at[5])
     pick = jnp.broadcast_to(mods[here][0:1, 0:1], (BLOCK, D)) == expert
     ghf[...] = jnp.where(pick, sb[own_rows, :], sr[...])
@@ -587,7 +519,7 @@
                 @pl.when(at_home)
                 def _():
                     pltpu.make_async_copy(
-                        fin.at[slot, s, e], finr.at[xlo, core, slot], fin_r.at[xlo, core, slot]
+                        fin.at[slot, s, e], finr.at[xlo, core, slot], fin_r.at[core]
                     ).start()
 
                 @pl.when(jnp.logical_not(at_home))
@@ -596,7 +528,7 @@
 
     def result_copy(slot, s, e):
         return send(
-            fin.at[slot, s, e], finr.at[xlo, core, slot], fin_s.at[slot, s, e], fin_r.at[xlo, core, slot],
+            fin.at[slot, s, e], finr.at[xlo, core, slot], fin_s.at[slot], fin_r.at[core],
             dp=s * 4 + y, mod=e,
         )
 
@@ -604,74 +536,50 @@
         last_leg(slot)
         results_out(slot)
 
-    lax.fori_loop(2, last - 1, each(second_leg), 0)
-    last_second_leg()
-    lax.fori_loop(core // 2, last - 1, each(last_step), 0)
-    last_last_leg()
-    results_out(last - 1)
+    lax.fori_loop(2, last, each(second_leg), 0)
+    lax.fori_loop(core // 2, last, each(last_step), 0)
 
     att_out.wait()
     gh_out.wait()
-    for g in range(2):
-        for c in range(2):
-            for slot in range(5 - c):
-                arrived(finr.at[g, c, slot], fin_r.at[g, c, slot])
+    arrived(finr.at[:, 0], fin_r.at[0])
+    arrived(finr.at[:, 1, 0:4], fin_r.at[1])
 
     for copy in sent:
         copy.wait_send()
 
-    def heads_sent(head, carry):
-        full_lanes = pl.ds(aligned(core * HEADS + head, HS), HS)
-        send(
-            attb.at[head, other_rows], attf.at[:, full_lanes], att_s.at[head], att_r.at[head], mod=other
-        ).wait_send()
-        send(dqb.at[head], gq.at[:, full_lanes], gq_s.at[head], gq_r.at[head], mod=other).wait_send()
-
-        @pl.when(jnp.logical_not(home))
-        def _():
-            cross(head).wait_send()
-
-        @pl.when(home)
-        def _():
-            fan_sent(dqb.at[head], xlo, head // 4, head % 4, b_s.at[0, head])
-            fan_sent(dqx.at[head], 1 - xlo, head // 4, head % 4, b_s.at[1, head])
-
+    arrived(attf.at[:, 0:GW], att_s)
+    arrived(gq.at[:, 0:GW], gq_s)
+    arrived(mods.at[0:15], mod_s)
+    arrived(kvall.at[:, 0:7 * CHIP], kv_s)
+    arrived(at.at[:, 0:8 * BLOCK], af_s)
+    arrived(at.at[:, 0:7 * BLOCK], a_s)
+    arrived(dkvb.at[0], dk_s.at[0])
+    arrived(dkr, dk_s.at[1])
+
+    @pl.when(jnp.logical_not(home))
+    def _():
+        arrived(dqb, bx_s)
+        arrived(bg.at[0], b_s.at[2])
+
+    @pl.when(home)
+    def _():
+        arrived(bg.at[0, 0:7 * CHIP], b_s.at[2])
+        for side in range(2):
+            @pl.when(core == 0)
+            def _():
+                arrived(bg.at[0:3], b_s.at[side])
+
+            @pl.when(core == 1)
+            def _():
+                arrived(bg.at[:, 0:5 * CHIP], b_s.at[side])
+
+    def blocks_sent(slot, carry):
+        arrived(cs.at[:, 0], c_s.at[slot])
+        arrived(cz.at[slot], cx_s.at[slot])
+        arrived(finr.at[0, 0, 0:3], fin_s.at[slot])
         return carry
 
-    lax.fori_loop(0, HEADS, heads_sent, 0)
-    for side in range(2):
-        for k in range(4):
-            pass_hidden(side, k).wait_send()
-            if side or k:
-                for s in range(2):
-                    hidden_copy(side, k, s).wait_send()
-    for i, target, slot in ((0, 0, 4), (1, 1, 3)):
-        straight_sent(gkv.at[i, core], target, slot, b_s.at[0, HEADS + i])
-
-    def blocks_sent(slot, carry):
-        then_x(slot).wait_send()
-        for k in (1, 3, 2):
-            z_leg(slot, k).wait_send()
-
-        @pl.when(slot < last - 1)
-        def _():
-            then_x1(slot).wait_send()
-            for k in (1, 3, 2):
-                z_leg1(slot, k).wait_send()
-
-        for s in range(2):
-            for e in range(2):
-
-                @pl.when(jnp.logical_not(jnp.logical_and(xlo == s, core == e)))
-                def _():
-                    result_copy(slot, s, e).wait_send()
-
-        return carry
-
     lax.fori_loop(0, last, blocks_sent, 0)
-    x_leg().wait_send()
-    for k in (1, 3, 2):
-        then_z(k).wait_send()
 
 
 def results(att, gh, fin, att_o, gh_o, gwq_o, gwkv_o):
@@ -698,14 +606,14 @@
         vmem((2, HS, SEQ), F32), vmem((2, 2, 4, HS, CHIP), BF), vmem((3, 2, HS, CHIP), BF), vmem((4, HS, CHIP), BF), vmem((4, HS, CHIP), BF), vmem((3, HS, CHIP), BF),
         vmem((HS, CHIP), BF), vmem((HS, CHIP), BF), vmem((2, 2, CHIP, HS), BF),
         vmem((5, SEQ, HS), BF), vmem((SEQ, 2 * HS), BF), vmem((2 * SLICE, 2 * HS), F32),
-        vmem((5, 4, 2, 2 * PART, HS), BF), vmem((5, 4, 2, 2 * PART, HS), BF), vmem((5, 3, 2, 2 * PART, HS), BF), vmem((5, 3, 2, 2 * PART, HS), BF), vmem((4, 2 * PART, HS), BF),
-        vmem((5, 2, 2 * PART, HS), BF), vmem((5, 2, 2 * PART, HS), BF), vmem((4, 2 * PART, HS), BF), vmem((3, 2 * PART, HS), BF), vmem((5, 2, 2 * PART, HS), F32),
+        vmem((5, 4, 2, 2 * PART, HS), BF), vmem((5, 4, 2, 2 * PART, HS), BF), vmem((5, 3, 2, 2 * PART, HS), BF), vmem((5, 4, 2 * PART, HS), BF),
+        vmem((5, 2 * PART, HS), BF), vmem((5, 2 * PART, HS), BF), vmem((5, 4, 2 * PART, HS), BF), vmem((5, 3, 2 * PART, HS), BF), vmem((5, 2, 2 * PART, HS), F32),
         vmem((5, 2, 2, 64, HS), BF),
         vmem((CHIP, D), BF), vmem((BLOCK, D), BF),
-        dma((11,)), dma((6,)), dma((6,)), dma((8, 2)), dma((8, 2)), dma((2, 4, 2)), dma((2, 4, 2)), dma((2, 4)), dma((2, 4)),
-        dma((2, 2, 4)), dma((2, 2, 4)), dma((HEADS,)), dma((HEADS,)), dma((HEADS,)), dma((HEADS,)),
-        dma((HEADS,)), dma((HEADS,)), dma((2, 9, 4)), dma((5, 8)), dma((8,)), dma((8,)), dma((5, 7)), dma((5, 7)), dma((6, 4)), dma((6, 4)),
-        dma((5, 2, 2)), dma((2, 2, 5)),
+        dma((11,)), dma((6,)), dma((6,)), dma(()), dma((2,)), dma(()), dma((2, 4)), dma(()), dma(()),
+        dma(()), dma((3,)), dma(()), dma(()), dma(()), dma(()),
+        dma(()), dma((HEADS,)), dma((3,)), dma((5,)), dma((2,)), dma((4,)), dma((5,)), dma((5, 2)), dma((5,)), dma((5, 2)),
+        dma((5,)), dma((2,)),
     ]
     in_vmem, anywhere = pl.BlockSpec(memory_space=pltpu.VMEM), pl.BlockSpec(memory_space=pl.ANY)
     raw = pl.pallas_call(

time: 86.7 us -> 83.6 us (0.964)
  Pallas kernels: 86 us -> 82.9 us
    pallas_call x1, Pallas kernels: 83.4 us -> 80.3 us  [on_device(): pl.pallas_call(layer, out_shape=(jax.ShapeDtypeStruct((BLOCK, QW), BF), j...]
where the time goes in v4:
time: 83.6 us; the launch traced here: 83.5 us
  Pallas kernels  82.9 us (99%)
    pallas_call x1, Pallas kernels, on_device(): pl.pallas_call(layer, out_shape=(jax.ShapeDtypeStruct((BLOCK, QW), BF), j...  80.3 us
    pallas_call x1, Pallas kernels, on_device(): pl.pallas_call(results, out_shape=(jax.ShapeDtypeStruct((BLOCK, QW), BF),...  2.59 us

profile of v4, /device:TPU:1, one launch (start us, length us, event | category | flops | bytes accessed | tf_op | source)
XLA Modules:
  0.0 83.5 jit_solution(11728465637966832150)
XLA Ops:
  0.6 80.3 %layer.1 = (bf16[128,1792]{1,0:T(8,128)(2,1)}, bf16[128,3584]{1,0:T(8,128)(2,1)}, bf16[2,2,5,64,128]{4,3,2,1,0:T(8,128)(2,1)}) custom-call(bf16[128,3584]{1,0:T(8,128)(2,1)} %bitcast.10, bf16[128,1792]{1,0:T(8,128)(2,1)} %bitcast.11, s32[1,128]{1,0:T(1,128)} %kinds_h.1, s32[1,2048]{1,0:T(1,128)} %segs_h.1, bf16[3584,1792]{1,0:T(8,128)(2,1)} %bitcast.8, ...), custom_call_target="tpu_custom_call" | custom-call | tf_op jit(solution)/shard_map/layer/pallas_call | solution.py:619
  80.9 2.6 %results.1 = (bf16[128,1792]{1,0:T(8,128)(2,1)}, bf16[128,3584]{1,0:T(8,128)(2,1)}, bf16[56,1792]{1,0:T(8,128)(2,1)}, bf16[56,512]{1,0:T(8,128)(2,1)}) custom-call(bf16[128,1792]{1,0:T(8,128)(2,1)} %get-tuple-element.11.att, bf16[128,3584]{1,0:T(8,128)(2,1)} %get-tuple-element.12.gh, bf16[2,2,5,64,128]{4,3,2,1,0:T(8,128)(2,1)} %get-tuple-element.13.fin), custom_call_target="tpu_custom_call" | custom-call | tf_op jit(solution)/shard_map/results/pallas_call | solution.py:634

commit v5 on v4

--- a/solution.py
+++ b/solution.py
@@ -47,9 +47,9 @@
     hid_h, og_h, kinds_h, segs_h, wq, wkv,
     att_o, gh_o, finr,
     hid, og, kinds, segs, attf, ghf, wq_v, wkv_v, hidf, hid_t, ogf, mods, at, kvs, kvr, kvall, qs, qr, qf, bias,
-    modv, attb, dqb, dqx, gq, acc, dkvb, dkr, dvr, dvz, dvzr, dkx, dkxr, gkv, bg, be, cf, cs, cs1, crz, crx, cx, cxr, cz, czr, keep, fin, sb, sr,
+    modv, attb, dqb, dqx, gq, acc, dkvb, dkr, dvr, dvz, dvzr, dkx, dkxr, gkv, gkvx, bg, be, cf, cs, cs1, crz, crx, cx, cxr, cz, czr, cl, crl, keep, fin, sb, sr,
     w_sem, pair_s, pair_r, mod_s, mod_r, a_s, a_r, af_s, af_r, kv_s, kv_r,
-    att_s, att_r, gq_s, gq_r, bx_s, bx_r, b_s, b_r, dk_s, dk_r, c_s, c_r, cx_s, cx_r, fin_s, fin_r,
+    att_s, att_r, gq_s, gq_r, bx_s, bx_r, kx, b_s, b_r, dk_s, dk_r, c_s, c_r, cx_s, cx_r, cl_s, cl_r, fin_s, fin_r,
 ):
     dp, ctx, core = lax.axis_index("dp"), lax.axis_index("ctx"), lax.axis_index("mod")
     xlo, y, xhi, z = dp // 4, dp % 4, ctx // 4, ctx % 4
@@ -75,12 +75,15 @@
         pl.semaphore_signal(barrier, inc=1, device_id={"dp": (dp + k) % 8, "mod": other}, device_id_type=MESH)
         if k:
             pl.semaphore_signal(barrier, inc=1, device_id={"dp": (dp + k) % 8}, device_id_type=MESH)
-            pl.semaphore_signal(barrier, inc=1, device_id={"ctx": (ctx + k) % 8}, device_id_type=MESH)
+            for side in range(2):
+                for c in range(2):
+                    to = {"dp": (1 - xlo if side else xlo) * 4 + y, "ctx": (ctx + k) % 8, "mod": other if c else core}
+                    pl.semaphore_signal(barrier, inc=1, device_id=to, device_id_type=MESH)
     for load in own_loads + loads:
         load.start()
     for load in own_loads:
         load.wait()
-    pl.semaphore_wait(barrier, 22)
+    pl.semaphore_wait(barrier, 43)
 
     own_rows = pl.ds(aligned(core, BLOCK), BLOCK)
     other_rows = pl.ds(aligned(other, BLOCK), BLOCK)
@@ -279,25 +282,8 @@
     def cross(head):
         return send(dqb.at[head], dqx.at[head], bx_s, bx_r.at[head], dp=(1 - xlo) * 4 + y)
 
-    def straight(src, target, slot, sems, k):
-        rows = pl.ds(aligned(dp, CHIP), CHIP)
-        return send(
-            src, bg.at[slot, rows], sems, b_r.at[slot], dp=core * 4 + (y + k) % 4, mod=target
-        )
-
-    def straight_out(src, target, slot, sems):
-        at_home = jnp.logical_and(home, target == core)
-        rows = pl.ds(aligned(dp, CHIP), CHIP)
-        for k in (1, 3, 2):
-            straight(src, target, slot, sems, k).start()
-
-        @pl.when(at_home)
-        def _():
-            pltpu.make_async_copy(src, bg.at[slot, rows], b_r.at[slot]).start()
-
-        @pl.when(jnp.logical_not(at_home))
-        def _():
-            straight(src, target, slot, sems, 0).start()
+    def cross_kv():
+        return send(gkv.at[:, core], gkvx, kx.at[0], kx.at[1], dp=(1 - xlo) * 4 + y)
 
     def fan(src, side, target, slot, sems, k):
         rows = pl.ds(pl.multiple_of((side * 4 + y) * CHIP, CHIP), CHIP)
@@ -333,7 +319,7 @@
         def _():
             fan_out(dqb.at[head], xlo, target, slot, b_s.at[0])
 
-    def block_sums(slot):
+    def products(slot):
         arrived(bg.at[slot], b_r.at[slot])
         for t in range(16):
             rows = slice(t * BLOCK, (t + 1) * BLOCK)
@@ -343,6 +329,9 @@
             be[rows, HS:] = second
             be[rows, :HS] = block - second
         cf[...] = dot(at[...], be[...])
+
+    def block_sums(slot):
+        products(slot)
         for c in range(8):
             for e, buf in enumerate((cs, cs1)):
                 cols = slice(e * HS, (e + 1) * HS)
@@ -388,6 +377,36 @@
             total += crz[slot, k, xhi].astype(F32)
         keep[slot, 0] = total
 
+    def straight_parts():
+        for c in range(8):
+            for e in range(2):
+                for s in range(2):
+                    part = cf[s * SLICE + c * PART:s * SLICE + (c + 1) * PART, e * HS:(e + 1) * HS]
+                    cl[c, e, s] = jnp.concatenate([part, jnp.zeros((8, HS), F32)], axis=0).astype(BF)
+
+    def part_copy(k, e, s):
+        to = (ctx + k) % 8
+        return send(
+            cl.at[to, e, s], crl.at[xlo * 2 + core, ctx], cl_s.at[0 if k else 1], cl_r, dp=s * 4 + y, ctx=to, mod=e
+        )
+
+    def send_parts():
+        for k in (4, 5, 7, 6, 1, 3, 2):
+            for e in range(2):
+                for s in range(2):
+                    part_copy(k, e, s).start()
+        for e in range(2):
+            for s in range(2):
+                own = jnp.logical_and(xlo == s, core == e)
+
+                @pl.when(own)
+                def _():
+                    pltpu.make_async_copy(cl.at[ctx, e, s], crl.at[xlo * 2 + core, ctx], cl_r).start()
+
+                @pl.when(jnp.logical_not(own))
+                def _():
+                    part_copy(0, e, s).start()
+
     def finish(slot, totals):
         for e, total in enumerate(totals):
             for s in range(2):
@@ -443,6 +462,12 @@
         return carry
 
     lax.fori_loop(0, 7, spread, 0)
+
+    @pl.when(home)
+    def _():
+        for i in (4, 5, 6):
+            relay_grads(i)
+
     arrived(at.at[:, 0:8 * BLOCK], af_r)
     other_kinds()
 
@@ -472,11 +497,6 @@
     dk_copy.start()
     first_leg(0)
     lax.fori_loop(1 + core // 2, 2, each(block_and_legs), 0)
-    @pl.when(home)
-    def _():
-        for i in (4, 5, 6):
-            relay_grads(i)
-
     dk = over_z(xhi)
     dv = acc[1, :, pl.ds(pl.multiple_of((xhi * 4 + z) * CHIP, CHIP), CHIP)] + dvr[z].astype(F32)
     arrived(dvzr, dk_r.at[2])
@@ -489,10 +509,23 @@
     gkv_copy = send(gkv.at[:, core], gkv.at[:, core], pair_s.at[4], pair_r.at[4], mod=other)
     gkv_copy.start()
     sent.append(gkv_copy)
-    for i, target, slot in ((0, 0, 4), (1, 1, 3)):
-        straight_out(gkv.at[i, core], target, slot, b_s.at[2])
+
+    @pl.when(jnp.logical_not(home))
+    def _():
+        cross_kv().start()
+
+    @pl.when(home)
+    def _():
+        for i, target, slot in ((0, 0, 4), (1, 1, 3)):
+            fan_out(gkv.at[i, core], xlo, target, slot, b_s.at[2])
 
     lax.fori_loop(2, last - 1, each(block_and_legs), 0)
+
+    @pl.when(home)
+    def _():
+        arrived(gkvx, kx.at[1])
+        for i, target, slot in ((0, 0, 4), (1, 1, 3)):
+            fan_out(gkvx.at[i], 1 - xlo, target, slot, b_s.at[2])
 
     arrived(gkv.at[:, other], pair_r.at[4])
     grads_kv = jnp.concatenate([gkv[0, 0], gkv[0, 1], gkv[1, 0], gkv[1, 1]], axis=1)
@@ -503,13 +536,15 @@
     home_copy = send(sb.at[other_rows], sr, pair_s.at[5], pair_r.at[5], mod=other)
     home_copy.start()
     sent.append(home_copy)
-    lax.fori_loop(last - 1, last, each(block_and_legs), 0)
+    lax.fori_loop(core // 2, last - 1, each(second_leg), 0)
+    lax.fori_loop(last - 1, last, each(products), 0)
+    straight_parts()
+    send_parts()
     arrived(sr, pair_r.at[5])
     pick = jnp.broadcast_to(mods[here][0:1, 0:1], (BLOCK, D)) == expert
     ghf[...] = jnp.where(pick, sb[own_rows, :], sr[...])
     gh_out = pltpu.make_async_copy(ghf, gh_o, w_sem.at[8])
     gh_out.start()
-    lax.fori_loop(0, 2, each(second_leg), 0)
 
     def results_out(slot):
         for s in range(2):
@@ -536,13 +571,19 @@
         last_leg(slot)
         results_out(slot)
 
-    lax.fori_loop(2, last, each(second_leg), 0)
-    lax.fori_loop(core // 2, last, each(last_step), 0)
+    lax.fori_loop(core // 2, last - 1, each(last_step), 0)
 
     att_out.wait()
     gh_out.wait()
-    arrived(finr.at[:, 0], fin_r.at[0])
-    arrived(finr.at[:, 1, 0:4], fin_r.at[1])
+    arrived(finr.at[:, 0, 0:4], fin_r.at[0])
+    arrived(finr.at[:, 1, 0:3], fin_r.at[1])
+    arrived(crl, cl_r)
+    for g in range(2):
+        for c in range(2):
+            total = crl[g * 2 + c, 0].astype(F32)
+            for source in range(1, 8):
+                total += crl[g * 2 + c, source].astype(F32)
+            finr[g, c, 4 - c] = total.astype(BF)
 
     for copy in sent:
         copy.wait_send()
@@ -559,11 +600,11 @@
     @pl.when(jnp.logical_not(home))
     def _():
         arrived(dqb, bx_s)
-        arrived(bg.at[0], b_s.at[2])
+        arrived(gkvx, kx.at[0])
 
     @pl.when(home)
     def _():
-        arrived(bg.at[0, 0:7 * CHIP], b_s.at[2])
+        arrived(bg.at[0:2, 0:7 * CHIP], b_s.at[2])
         for side in range(2):
             @pl.when(core == 0)
             def _():
@@ -579,7 +620,9 @@
         arrived(finr.at[0, 0, 0:3], fin_s.at[slot])
         return carry
 
-    lax.fori_loop(0, last, blocks_sent, 0)
+    lax.fori_loop(0, last - 1, blocks_sent, 0)
+    arrived(cl.at[0:7], cl_s.at[0])
+    arrived(finr.at[0, 0, 0:3], cl_s.at[1])
 
 
 def results(att, gh, fin, att_o, gh_o, gwq_o, gwkv_o):
@@ -604,16 +647,16 @@
         vmem((2, CHIP, GW), BF), vmem((CHIP, GW), BF), vmem((CHIP, GW), BF), vmem((CHIP, SEQ), F32),
         vmem((8, BLOCK), F32), vmem((HEADS, CHIP, HS), BF), vmem((HEADS, CHIP, HS), BF), vmem((HEADS, CHIP, HS), BF), vmem((CHIP, QW), BF),
         vmem((2, HS, SEQ), F32), vmem((2, 2, 4, HS, CHIP), BF), vmem((3, 2, HS, CHIP), BF), vmem((4, HS, CHIP), BF), vmem((4, HS, CHIP), BF), vmem((3, HS, CHIP), BF),
-        vmem((HS, CHIP), BF), vmem((HS, CHIP), BF), vmem((2, 2, CHIP, HS), BF),
+        vmem((HS, CHIP), BF), vmem((HS, CHIP), BF), vmem((2, 2, CHIP, HS), BF), vmem((2, CHIP, HS), BF),
         vmem((5, SEQ, HS), BF), vmem((SEQ, 2 * HS), BF), vmem((2 * SLICE, 2 * HS), F32),
         vmem((5, 4, 2, 2 * PART, HS), BF), vmem((5, 4, 2, 2 * PART, HS), BF), vmem((5, 3, 2, 2 * PART, HS), BF), vmem((5, 4, 2 * PART, HS), BF),
-        vmem((5, 2 * PART, HS), BF), vmem((5, 2 * PART, HS), BF), vmem((5, 4, 2 * PART, HS), BF), vmem((5, 3, 2 * PART, HS), BF), vmem((5, 2, 2 * PART, HS), F32),
+        vmem((5, 2 * PART, HS), BF), vmem((5, 2 * PART, HS), BF), vmem((5, 4, 2 * PART, HS), BF), vmem((5, 3, 2 * PART, HS), BF), vmem((8, 2, 2, 64, HS), BF), vmem((4, 8, 64, HS), BF), vmem((5, 2, 2 * PART, HS), F32),
         vmem((5, 2, 2, 64, HS), BF),
         vmem((CHIP, D), BF), vmem((BLOCK, D), BF),
         dma((11,)), dma((6,)), dma((6,)), dma(()), dma((2,)), dma(()), dma((2, 4)), dma(()), dma(()),
         dma(()), dma((3,)), dma(()), dma(()), dma(()), dma(()),
-        dma(()), dma((HEADS,)), dma((3,)), dma((5,)), dma((2,)), dma((4,)), dma((5,)), dma((5, 2)), dma((5,)), dma((5, 2)),
-        dma((5,)), dma((2,)),
+        dma(()), dma((HEADS,)), dma((2,)), dma((3,)), dma((5,)), dma((2,)), dma((4,)), dma((5,)), dma((5, 2)), dma((5,)), dma((5, 2)),
+        dma((2,)), dma(()), dma((5,)), dma((2,)),
     ]
     in_vmem, anywhere = pl.BlockSpec(memory_space=pltpu.VMEM), pl.BlockSpec(memory_space=pl.ANY)
     raw = pl.pallas_call(

time: 83.6 us -> 81.1 us (0.970)
  Pallas kernels: 82.9 us -> 80.3 us
    pallas_call x1, Pallas kernels: 80.3 us -> 77.7 us  [on_device(): pl.pallas_call(layer, out_shape=(jax.ShapeDtypeStruct((BLOCK, QW), BF), j...]
where the time goes in v5:
time: 81.1 us; the launch traced here: 80.9 us
  Pallas kernels  80.3 us (99%)
    pallas_call x1, Pallas kernels, on_device(): pl.pallas_call(layer, out_shape=(jax.ShapeDtypeStruct((BLOCK, QW), BF), j...  77.7 us
    pallas_call x1, Pallas kernels, on_device(): pl.pallas_call(results, out_shape=(jax.ShapeDtypeStruct((BLOCK, QW), BF),...  2.59 us

profile of v5, /device:TPU:1, one launch (start us, length us, event | category | flops | bytes accessed | tf_op | source)
XLA Modules:
  0.0 80.9 jit_solution(16388369874705210520)
XLA Ops:
  0.6 77.7 %layer.1 = (bf16[128,1792]{1,0:T(8,128)(2,1)}, bf16[128,3584]{1,0:T(8,128)(2,1)}, bf16[2,2,5,64,128]{4,3,2,1,0:T(8,128)(2,1)}) custom-call(bf16[128,3584]{1,0:T(8,128)(2,1)} %bitcast.10, bf16[128,1792]{1,0:T(8,128)(2,1)} %bitcast.11, s32[1,128]{1,0:T(1,128)} %kinds_h.1, s32[1,2048]{1,0:T(1,128)} %segs_h.1, bf16[3584,1792]{1,0:T(8,128)(2,1)} %bitcast.8, ...), custom_call_target="tpu_custom_call" | custom-call | tf_op jit(solution)/shard_map/layer/pallas_call | solution.py:662
  78.3 2.6 %results.1 = (bf16[128,1792]{1,0:T(8,128)(2,1)}, bf16[128,3584]{1,0:T(8,128)(2,1)}, bf16[56,1792]{1,0:T(8,128)(2,1)}, bf16[56,512]{1,0:T(8,128)(2,1)}) custom-call(bf16[128,1792]{1,0:T(8,128)(2,1)} %get-tuple-element.11.att, bf16[128,3584]{1,0:T(8,128)(2,1)} %get-tuple-element.12.gh, bf16[2,2,5,64,128]{4,3,2,1,0:T(8,128)(2,1)} %get-tuple-element.13.fin), custom_call_target="tpu_custom_call" | custom-call | tf_op jit(solution)/shard_map/results/pallas_call | solution.py:677

commit v6 on v5

--- a/solution.py
+++ b/solution.py
@@ -113,7 +113,7 @@
         to = (y + k) % 4
         rows = pl.ds(pl.multiple_of((s * 4 + to) * SLICE, 64), SLICE)
         return send(
-            hid_t.at[rows], at.at[pl.ds(s * SLICE, SLICE), here_lanes], a_s, a_r.at[side, k],
+            hid_t.at[rows], at.at[pl.ds(s * SLICE, SLICE), here_lanes], a_s, a_r.at[side],
             dp=(xlo if side == 0 else 1 - xlo) * 4 + to,
         )
 
@@ -135,8 +135,6 @@
         return send(at.at[:, lanes], at.at[:, lanes], af_s, af_r, mod=other)
 
     def relay_hidden(side, k):
-        if side or k:
-            arrived(at.at[:, lanes_of(side, k)], a_r.at[side, k])
         pass_hidden(side, k).start()
 
     loads[0].wait()
@@ -262,16 +260,19 @@
 
         @pl.when(jnp.logical_and(home, p == 2))
         def _():
+            arrived(dqx.at[0:2], bx_r.at[0])
             relay_grads(0)
             relay_grads(1)
 
         @pl.when(p == 1)
         def _():
+            arrived(at.at[:, 0:3 * BLOCK], a_r.at[0])
             for k in range(4):
                 relay_hidden(0, k)
 
         @pl.when(p == 2)
         def _():
+            arrived(at.at[:, 0:4 * BLOCK], a_r.at[1])
             for k in (0, 2, 1, 3):
                 relay_hidden(1, k)
 
@@ -280,7 +281,7 @@
     home = xlo == core
 
     def cross(head):
-        return send(dqb.at[head], dqx.at[head], bx_s, bx_r.at[head], dp=(1 - xlo) * 4 + y)
+        return send(dqb.at[head], dqx.at[head], bx_s, bx_r.at[head % 4 - head % 4 // 3], dp=(1 - xlo) * 4 + y)
 
     def cross_kv():
         return send(gkv.at[:, core], gkvx, kx.at[0], kx.at[1], dp=(1 - xlo) * 4 + y)
@@ -307,7 +308,6 @@
     def relay_grads(i):
         slot, target = i // 2, i % 2
         head = target * 4 + slot
-        arrived(dqx.at[head], bx_r.at[head])
         fan_out(dqx.at[head], 1 - xlo, target, slot, b_s.at[1])
 
     def spread_grads(head, target, slot):
@@ -445,6 +445,7 @@
 
     @pl.when(home)
     def _():
+        arrived(dqx.at[0:2], bx_r.at[1])
         for i in (2, 3):
             relay_grads(i)
 
@@ -465,6 +466,7 @@
 
     @pl.when(home)
     def _():
+        arrived(dqx.at[0:3], bx_r.at[2])
         for i in (4, 5, 6):
             relay_grads(i)
 
@@ -653,10 +655,10 @@
         vmem((5, 2 * PART, HS), BF), vmem((5, 2 * PART, HS), BF), vmem((5, 4, 2 * PART, HS), BF), vmem((5, 3, 2 * PART, HS), BF), vmem((8, 2, 2, 64, HS), BF), vmem((4, 8, 64, HS), BF), vmem((5, 2, 2 * PART, HS), F32),
         vmem((5, 2, 2, 64, HS), BF),
         vmem((CHIP, D), BF), vmem((BLOCK, D), BF),
-        dma((11,)), dma((6,)), dma((6,)), dma(()), dma((2,)), dma(()), dma((2, 4)), dma(()), dma(()),
+        dma((11,)), dma((6,)), dma((6,)), dma(()), dma((2,)), dma(()), dma((2,)), dma(()), dma(()),
         dma(()), dma((3,)), dma(()), dma(()), dma(()), dma(()),
-        dma(()), dma((HEADS,)), dma((2,)), dma((3,)), dma((5,)), dma((2,)), dma((4,)), dma((5,)), dma((5, 2)), dma((5,)), dma((5, 2)),
-        dma((2,)), dma(()), dma((5,)), dma((2,)),
+        dma(()), dma((3,)), dma((2,)), dma((3,)), dma((5,)), dma((2,)), dma((4,)), dma((4,)), dma((4, 2)), dma((4,)), dma((4, 2)),
+        dma((2,)), dma(()), dma((4,)), dma((2,)),
     ]
     in_vmem, anywhere = pl.BlockSpec(memory_space=pltpu.VMEM), pl.BlockSpec(memory_space=pl.ANY)
     raw = pl.pallas_call(

time: 81.1 us -> 80.9 us (level)
  no operation moved by 1% of the time
where the time goes in v6:
time: 80.9 us; the launch traced here: 80.8 us
  Pallas kernels  80.1 us (99%)
    pallas_call x1, Pallas kernels, on_device(): pl.pallas_call(layer, out_shape=(jax.ShapeDtypeStruct((BLOCK, QW), BF), j...  77.6 us
    pallas_call x1, Pallas kernels, on_device(): pl.pallas_call(results, out_shape=(jax.ShapeDtypeStruct((BLOCK, QW), BF),...  2.59 us

profile of v6, /device:TPU:1, one launch (start us, length us, event | category | flops | bytes accessed | tf_op | source)
XLA Modules:
  0.0 80.8 jit_solution(10851332548206985183)
XLA Ops:
  0.6 77.6 %layer.1 = (bf16[128,1792]{1,0:T(8,128)(2,1)}, bf16[128,3584]{1,0:T(8,128)(2,1)}, bf16[2,2,5,64,128]{4,3,2,1,0:T(8,128)(2,1)}) custom-call(bf16[128,3584]{1,0:T(8,128)(2,1)} %bitcast.10, bf16[128,1792]{1,0:T(8,128)(2,1)} %bitcast.11, s32[1,128]{1,0:T(1,128)} %kinds_h.1, s32[1,2048]{1,0:T(1,128)} %segs_h.1, bf16[3584,1792]{1,0:T(8,128)(2,1)} %bitcast.8, ...), custom_call_target="tpu_custom_call" | custom-call | tf_op jit(solution)/shard_map/layer/pallas_call | solution.py:664
  78.2 2.6 %results.1 = (bf16[128,1792]{1,0:T(8,128)(2,1)}, bf16[128,3584]{1,0:T(8,128)(2,1)}, bf16[56,1792]{1,0:T(8,128)(2,1)}, bf16[56,512]{1,0:T(8,128)(2,1)}) custom-call(bf16[128,1792]{1,0:T(8,128)(2,1)} %get-tuple-element.11.att, bf16[128,3584]{1,0:T(8,128)(2,1)} %get-tuple-element.12.gh, bf16[2,2,5,64,128]{4,3,2,1,0:T(8,128)(2,1)} %get-tuple-element.13.fin), custom_call_target="tpu_custom_call" | custom-call | tf_op jit(solution)/shard_map/results/pallas_call | solution.py:679
